TPU v7x, 32 devices: a whole 2x2x4 slice. The times are simulated.
32 devices in a mesh: seq: 8 (over z, y), ch: 4 (over x, core).
Axes of the slice: x: 2, y: 2, z: 4, core: 2. Of those that a mesh axis runs over, the one named last changes fastest.
Arguments:
- signal_x: bfloat16 [64, 4096], P('ch', 'seq'), may hold values from -6 to 6
- gate_q: bfloat16 [64, 4096], P('ch', 'seq'), may hold values from -6 to 6
- gate_k: bfloat16 [64, 4096], P('ch', 'seq'), may hold values from -6 to 6
- skip_gain: float32 [64], P('ch'), may hold values from 0.5 to 1.5
- residue: float32 [16], replicated, may hold values from -1.5 to 1.5
- memory: float32 [16], replicated, may hold values from 30 to 16384
- cotangent: bfloat16 [64, 4096], P('ch', 'seq'), may hold values from -6 to 6
Outputs:
- output: bfloat16 [64, 4096], P('ch', 'seq')
- grad_x: bfloat16 [64, 4096], P('ch', 'seq')
- grad_q: bfloat16 [64, 4096], P('ch', 'seq')
- grad_k: bfloat16 [64, 4096], P('ch', 'seq')
- grad_skip: float32 [64], P('ch')
- grad_residue: float32 [16], replicated
- grad_memory: float32 [16], replicated
All inputs are finite; a program needn't handle non-finite values.
Results may differ from a plain program's by a relative error of at most 0.002.
Values sent between devices are 32-bit elements; how exact they have to be, the bound alone decides.
No kernel may reach another device: no remote copies, remote signals or barrier semaphores. Data moves between devices by JAX's collectives and lax.ppermute only.
A program may use at most 64 MiB of HBM per device.

v0:
```python
import functools
import math

import jax
import jax.numpy as jnp
from jax import lax
from jax.experimental import pallas as pl
from jax.experimental.pallas import tpu as pltpu
from jax.sharding import PartitionSpec as P

F32 = jnp.float32
BF16 = jnp.bfloat16
LANES = 128


def iota(shape, dim):
    return lax.broadcasted_iota(jnp.int32, shape, dim)


def roll(data, shift):
    return pltpu.roll(data, shift % LANES, 1)


def nt_dot(left, right):
    return lax.dot_general(left, right, (((1,), (1,)), ((), ())), preferred_element_type=F32)


def nn_dot(left, right):
    return lax.dot_general(left, right, (((1,), (0,)), ((), ())), preferred_element_type=F32)


def tn_dot(left, right):
    return lax.dot_general(left, right, (((0,), (0,)), ((), ())), preferred_element_type=F32)


def halves(data):
    high = data.astype(BF16)
    return high, (data - high.astype(F32)).astype(BF16)


def left_split(data):
    high, low = halves(data)
    return jnp.concatenate([high, low, high], axis=1)


def right_split(data, axis=1):
    high, low = halves(data)
    return jnp.concatenate([high, high, low], axis=axis)


def by_chunk(ref):
    chunks = ref.shape[1] // LANES
    return jnp.concatenate([ref[:, j * LANES : (j + 1) * LANES].astype(F32) for j in range(chunks)], axis=0)


def column(row):
    size = row.shape[1]
    square = jnp.broadcast_to(row, (size, size))
    return jnp.sum(jnp.where(iota((size, size), 0) == iota((size, size), 1), square, 0.0), axis=1, keepdims=True)


def tiled_row(col):
    size = col.shape[0]
    spread = jnp.where(iota((size, LANES), 1) % size == iota((size, LANES), 0), col, 0.0)
    return jnp.sum(spread, axis=0, keepdims=True)


def decays(inv_col):
    modes = inv_col.shape[0]
    offset = iota((modes, LANES), 1).astype(F32)
    age_in = (LANES - offset) * inv_col
    age_out = offset * inv_col
    return jnp.exp(-age_in), age_in, jnp.exp(-age_out), age_out


def pad_rows(data):
    return jnp.concatenate([data, jnp.zeros((LANES - data.shape[0], data.shape[1]), data.dtype)], axis=0)


def make_states(*refs):
    sources, (out_ref, *copies), arrived = refs[:7], refs[7:15], refs[15]
    moves = [pltpu.make_async_copy(*ends, arrived.at[i]) for i, ends in enumerate(zip(sources, copies))]
    for move in moves:
        move.start()
    for move in moves:
        move.wait()
    memory_ref, _, _, x_ref, q_ref, k_ref, d_ref = copies
    modes = memory_ref.shape[1]
    channels, local_len = x_ref.shape
    chunks = local_len // LANES
    inv_col = column(1.0 / memory_ref[...])
    inv_row = tiled_row(inv_col)
    decay_in, age_in, decay_out, age_out = decays(inv_col)
    values = by_chunk(x_ref) * by_chunk(k_ref)
    grads = by_chunk(d_ref) * by_chunk(q_ref)
    value_split = left_split(values)
    grad_split = left_split(grads)
    first_in, first_out = decay_in * age_in, decay_out * age_out
    pair = jnp.concatenate(
        [
            pad_rows(jnp.concatenate([decay_in, first_in], axis=0)),
            pad_rows(jnp.concatenate([first_in, decay_in], axis=0)),
        ],
        axis=0,
    )
    value_states = nt_dot(value_split, right_split(pair))
    grad_states = nt_dot(grad_split, right_split(pad_rows(jnp.concatenate([decay_out, first_out], axis=0))))
    lane = iota((channels, LANES), 1)
    step = jnp.exp(-LANES * inv_row)
    growth = LANES * inv_row
    growth_low = jnp.where(lane < modes, growth, 0.0)
    growth_high = jnp.where((lane >= modes) & (lane < 2 * modes), growth, 0.0)
    prefix = jnp.zeros((channels, LANES), F32)
    swapped = prefix
    cross_zero = prefix
    cross_one = prefix
    suffix = prefix
    weighted = prefix
    power = jnp.ones_like(step)
    for j in range(chunks):
        rows = slice(j * channels, (j + 1) * channels)
        grad_part = grad_states[rows]
        if j > 0:
            cross_zero = cross_zero + prefix * grad_part
            cross_one = cross_one + swapped * grad_part
        prefix, swapped = (
            step * (prefix + growth_high * swapped) + value_states[rows, :LANES],
            step * (swapped + growth_low * prefix) + value_states[rows, LANES:],
        )
        suffix = suffix + power * grad_part
        weighted = weighted + (j * power) * grad_part
        power = power * step
    suffix = suffix + growth_high * roll(weighted, modes)
    pack = jnp.where(lane < 2 * modes, prefix, 0.0) + roll(jnp.where(lane < 2 * modes, suffix, 0.0), 2 * modes)
    half = channels // 2
    payload = pack[:half] + roll(pack[half:], 4 * modes)
    high_v, low_v = halves(values)
    high_g, low_g = halves(grads)
    outer = tn_dot(
        jnp.concatenate([high_v, low_v, high_v], axis=0), jnp.concatenate([high_g, high_g, low_g], axis=0)
    )
    outer = jnp.where(iota(outer.shape, 1) >= iota(outer.shape, 0), outer, 0.0)
    turn = (iota(outer.shape, 1) + iota(outer.shape, 0)) % LANES
    skewed = jnp.take_along_axis(outer, turn, axis=1, mode="promise_in_bounds")
    by_distance = jnp.sum(skewed, axis=0, keepdims=True)
    near = decay_out * by_distance
    near_zero = jnp.sum(near, axis=1, keepdims=True)
    near_one = jnp.sum(near * age_out, axis=1, keepdims=True)
    products = values * grads
    part_skip = products[:channels]
    for j in range(1, chunks):
        part_skip = part_skip + products[j * channels : (j + 1) * channels]
    part_skip = jnp.sum(part_skip, axis=1, keepdims=True)
    row_id = iota((channels, LANES), 0)
    extras = (
        jnp.where(lane < modes, cross_zero, 0.0)
        + roll(jnp.where(lane < 2 * modes, cross_one, 0.0), modes)
        + jnp.where(lane == row_id, near_zero, 0.0)
        + jnp.where(lane == row_id + modes, near_one, 0.0)
        + jnp.where(lane == row_id + 3 * modes, part_skip, 0.0)
    )
    for i in range(half):
        out_ref[i] = payload[i : i + 1]
    out_ref[half] = jnp.sum(extras, axis=0, keepdims=True)


def finish(seq_size, ch_size, memory_ref, residue_ref, skip_ref, x_ref, q_ref, k_ref, d_ref, all_ref,
           *refs):
    results, scratch, sent = refs[:7], refs[7:14], refs[14]
    output_ref, grad_x_ref, grad_q_ref, grad_k_ref, grad_skip_ref, grad_residue_ref, grad_memory_ref = scratch
    moves = [pltpu.make_async_copy(*ends, sent.at[i]) for i, ends in enumerate(zip(scratch, results))]
    modes = memory_ref.shape[1]
    channels, local_len = x_ref.shape
    chunks = local_len // LANES
    half = channels // 2
    me_seq, me_ch = lax.axis_index("seq"), lax.axis_index("ch")
    inv = 1.0 / memory_ref[...]
    inv_col = column(inv)
    inv_row = tiled_row(inv_col)
    decay_in, _, decay_out, _ = decays(inv_col)
    amplitude = column(residue_ref[...] * jnp.sqrt(2.0 * inv))
    signal, gate_out = by_chunk(x_ref), by_chunk(q_ref)
    gate_in, cotangent = by_chunk(k_ref), by_chunk(d_ref)
    values = signal * gate_in
    grads = cotangent * gate_out
    value_split = left_split(values)
    grad_split = left_split(grads)

    leap = jnp.exp(-local_len * inv_row)
    lane = iota((half, LANES), 1)

    def block(device):
        return all_ref[device, :half, 0, :]

    def before(d, carry):
        return jnp.where(d < me_seq, leap * carry + block(d * ch_size + me_ch), carry)

    def after(i, carry):
        d = seq_size - 1 - i
        return jnp.where(d > me_seq, leap * carry + block(d * ch_size + me_ch), carry)

    def loop(body, init):
        if seq_size <= 8:
            for i in range(seq_size):
                init = body(i, init)
            return init
        return lax.fori_loop(0, seq_size, body, init)

    zeros = jnp.zeros((half, LANES), F32)
    border_v = loop(before, zeros)
    border_g = roll(loop(after, zeros), -2 * modes)

    def three_times(data):
        full = jnp.concatenate([data, roll(data, -4 * modes)], axis=0)
        full = jnp.where(iota(full.shape, 1) < modes, full, 0.0)
        return full + roll(full, modes) + roll(full, 2 * modes)

    border_v, border_g = three_times(border_v), three_times(border_g)

    thrice_in = pad_rows(jnp.concatenate([decay_in] * 3, axis=0))
    thrice_out = pad_rows(jnp.concatenate([decay_out] * 3, axis=0))
    value_states = nt_dot(value_split, right_split(thrice_in))
    grad_states = nt_dot(grad_split, right_split(thrice_out))
    step = jnp.exp(-LANES * inv_row)
    starts, ends = [border_v], [border_g]
    for j in range(chunks - 1):
        starts.append(step * starts[-1] + value_states[j * channels : (j + 1) * channels])
        i = chunks - 1 - j
        ends.append(step * ends[-1] + grad_states[i * channels : (i + 1) * channels])
    rows = chunks * channels
    tail = iota((rows, LANES), 1) >= 2 * modes

    def state_split(parts):
        data = jnp.concatenate(parts, axis=0)
        high = data.astype(BF16).astype(F32)
        return jnp.where(tail, data - high, high).astype(BF16)

    def readout(decay):
        high, low = halves(amplitude * decay)
        return pad_rows(jnp.concatenate([high, low, high], axis=0))

    taps = jnp.sum(amplitude * decay_out, axis=0, keepdims=True)
    toeplitz = pltpu.roll(jnp.broadcast_to(taps, (LANES, LANES)), 0, 1, stride=1, stride_axis=0)
    square = (LANES, LANES)
    toeplitz = jnp.where(iota(square, 1) >= iota(square, 0), toeplitz, 0.0)
    conv = nn_dot(value_split, right_split(toeplitz, axis=0)) + nn_dot(state_split(starts), readout(decay_out))
    corr = nt_dot(grad_split, right_split(toeplitz)) + nn_dot(state_split(ends[::-1]), readout(decay_in))
    gain = jnp.concatenate([column(skip_ref[...])] * chunks, axis=0)
    mixed = conv + gain * values
    grad_values = gain * grads + corr

    for i, data in enumerate((gate_out * mixed, grad_values * gate_in, cotangent * mixed, grad_values * signal)):
        for j in range(chunks):
            scratch[i][:, j * LANES : (j + 1) * LANES] = data[j * channels : (j + 1) * channels].astype(BF16)
        moves[i].start()

    kind = iota((ch_size * half, LANES), 1) // modes % 4
    growth = local_len * inv_row
    growth_low = jnp.where(kind == 0, growth, 0.0)
    growth_high = jnp.where(kind == 1, growth, 0.0)

    def pairs(e, carry):
        prefix, swapped, cross_zero, cross_one, extras = carry
        state = jnp.concatenate([block(e * ch_size + c) for c in range(ch_size)], axis=0)
        turned = jnp.where(kind == 0, roll(state, -modes), roll(state, modes))
        grad_part = roll(state, -2 * modes)
        for c in range(ch_size):
            extras = extras + all_ref[e * ch_size + c, half]
        return (
            leap * (prefix + growth_high * swapped) + state,
            leap * (swapped + growth_low * prefix) + turned,
            cross_zero + prefix * grad_part,
            cross_one + swapped * grad_part,
            extras,
        )

    wide = jnp.zeros((ch_size * half, LANES), F32)
    _, _, cross_zero, cross_one, extras = loop(pairs, (wide, wide, wide, wide, jnp.zeros((1, LANES), F32)))
    cross_zero = jnp.sum(jnp.where(kind == 0, cross_zero, 0.0), axis=0, keepdims=True)
    cross_one = jnp.sum(jnp.where(kind <= 1, cross_one, 0.0), axis=0, keepdims=True)
    cross_one = cross_one + roll(cross_one, -modes)
    sum_zero = extras + cross_zero + roll(cross_zero, -4 * modes)
    sum_one = roll(extras, -modes) + roll(extras, -2 * modes) + cross_one + roll(cross_one, -4 * modes)
    sum_zero, sum_one = sum_zero[:, :modes], sum_one[:, :modes]
    scale = jnp.sqrt(2.0 * inv) / math.sqrt(ch_size * channels * seq_size * local_len)
    grad_residue_ref[...] = scale * sum_zero
    grad_memory_ref[...] = residue_ref[...] * scale * (sum_one - 0.5 * sum_zero)

    def skips(d, carry):
        return carry + all_ref[d * ch_size + me_ch, half]

    skip_sum = roll(loop(skips, jnp.zeros((1, LANES), F32)), -3 * modes)
    grad_skip_ref[...] = skip_sum[:, :channels] / math.sqrt(seq_size * local_len)
    for move in moves[4:]:
        move.start()
    for move in moves:
        move.wait()


def per_device(signal_x, gate_q, gate_k, skip_gain, residue, memory, cotangent):
    channels, local_len = signal_x.shape
    modes = memory.shape[0]
    seq_size, ch_size = lax.axis_size("seq"), lax.axis_size("ch")
    devices = seq_size * ch_size
    params = pltpu.CompilerParams(vmem_limit_bytes=32 * 1024 * 1024)
    rows = channels // 2 + 1
    arguments = (memory[None], residue[None], skip_gain[None], signal_x, gate_q, gate_k, cotangent)
    arguments = [pltpu.with_memory_space_constraint(data, pltpu.HBM) for data in arguments]
    in_hbm = pl.BlockSpec(memory_space=pltpu.HBM)
    mine, *here = pl.pallas_call(
        make_states,
        in_specs=[in_hbm] * 7,
        out_shape=(
            jax.ShapeDtypeStruct((rows, 1, LANES), F32),
            *[jax.ShapeDtypeStruct(data.shape, data.dtype) for data in arguments],
        ),
        scratch_shapes=[pltpu.SemaphoreType.DMA((7,))],
        compiler_params=params,
    )(*arguments)
    everyone = lax.all_to_all(jnp.broadcast_to(mine[None], (devices, rows, 1, LANES)), ("seq", "ch"), 0, 0)
    big = ((channels, local_len), BF16)
    shapes = [big] * 4 + [((1, channels), F32), ((1, modes), F32), ((1, modes), F32)]
    results = pl.pallas_call(
        functools.partial(finish, seq_size, ch_size),
        out_shape=[jax.ShapeDtypeStruct(*shape) for shape in shapes],
        out_specs=[in_hbm] * 7,
        scratch_shapes=[*[pltpu.VMEM(*shape) for shape in shapes], pltpu.SemaphoreType.DMA((7,))],
        compiler_params=params,
    )(*here, everyone)
    return (*results[:4], *[result[0] for result in results[4:]])


def solution(mesh):
    grid = P("ch", "seq")
    return jax.shard_map(
        per_device,
        mesh=mesh,
        in_specs=(grid, grid, grid, P("ch"), P(), P(), grid),
        out_specs=(grid, grid, grid, grid, P("ch"), P(), P()),
        check_vma=False,
    )
```

profile of v0, /device:TPU:0, one launch (start us, length us, event | category | flops | bytes accessed | tf_op | source)
XLA Modules:
  0.0 18.9 jit_solution(16508739764384349909)
XLA Ops:
  0.6 1.4 %shard_map.126 = (f32[9,1,128]{2,1,0:T(1,128)S(1)}, f32[1,16]{1,0:T(1,128)S(1)}, f32[1,16]{1,0:T(1,128)S(1)}, f32[1,16]{1,0:T(1,128)S(1)}, bf16[16,512]{1,0:T(8,...) custom-call(f32[1,16]{1,0:T(1,128)} %bitcast.10, ...), custom_call_target="tpu_custom_call" | custom-call | tf_op jit(solution)/shard_map/pallas_call | solution.py:310
  2.1 0.1 broadcast_in_dim.21
  2.1 15.5 %all_to_all.5.all_ref = f32[32,9,1,128]{3,2,1,0:T(1,128)S(1)} all-to-all(f32[32,9,1,128]{3,2,1,0:T(1,128)S(1)} %broadcast_in_dim.21), channel_id=1, replica_groups=mesh['seq'=8,'ch'=4] {'seq','ch'}, dimensions={0} | all-to-all | bytes 294912 | tf_op jit(solution)/shard_map/all_to_all | solution.py:320
  17.7 1.2 %shard_map.127 = (bf16[16,512]{1,0:T(8,128)(2,1)}, bf16[16,512]{1,0:T(8,128)(2,1)}, bf16[16,512]{1,0:T(8,128)(2,1)}, bf16[16,512]{1,0:T(8,128)(2,1)}, f32[1,16]{...) custom-call(f32[1,16]{1,0:T(1,128)S(1)} %get-tuple-element.22.memory_ref, f32[1,16]{1,0:T(1,128)S(1)} %get-tuple-element.23.residue_ref, ...), custom_call_target="tpu_custom_call" | custom-call | tf_op jit(solution)/shard_map/pallas_call | solution.py:323
  (1 shorter events, 0.0 us)
where the time goes:
time: 19.1 us; the launch traced here: 18.9 us
  blocking collectives  15.5 us (81%)
  Pallas kernels  2.64 us (14%)
  between operations  0.66 us (3%)
    all_to_all x1, blocking collectives, per_device(): lax.all_to_all(jnp.broadcast_to(mine[None], (devices, rows, 1, LANES)), (...  15.5 us
    pallas_call x1, Pallas kernels, per_device(): pl.pallas_call(make_states, in_specs=[in_hbm] * 7, out_shape=(jax.ShapeDt...  1.4 us
    pallas_call x1, Pallas kernels, per_device(): pl.pallas_call(functools.partial(finish, seq_size, ch_size), out_shape=[j...  1.24 us

commit v1 on v0

v1 whole, which is shorter than its diff:
```python
import functools
import math

import jax
import jax.numpy as jnp
from jax import lax
from jax.experimental import pallas as pl
from jax.experimental.pallas import tpu as pltpu
from jax.sharding import PartitionSpec as P

F32 = jnp.float32
BF16 = jnp.bfloat16
LANES = 128
AXES = ("ch", "seq")


def iota(shape, dim):
    return lax.broadcasted_iota(jnp.int32, shape, dim)


def roll(data, shift):
    return pltpu.roll(data, shift % LANES, 1)


def contract(left, right, left_dim, right_dim):
    dims = (((left_dim,), (right_dim,)), ((), ()))
    return lax.dot_general(left, right, dims, preferred_element_type=F32)


def halves(data):
    high = data.astype(BF16)
    return high, (data - high.astype(F32)).astype(BF16)


def left_split(data, axis=1):
    high, low = halves(data)
    return jnp.concatenate([high, low, high], axis=axis)


def right_split(data, axis=1):
    high, low = halves(data)
    return jnp.concatenate([high, high, low], axis=axis)


def by_chunk(ref):
    chunks = ref.shape[1] // LANES
    return jnp.concatenate([ref[:, j * LANES : (j + 1) * LANES].astype(F32) for j in range(chunks)], axis=0)


def column(row):
    size = row.shape[1]
    square = jnp.broadcast_to(row, (size, size))
    return jnp.sum(jnp.where(iota((size, size), 0) == iota((size, size), 1), square, 0.0), axis=1, keepdims=True)


def tiled_row(col):
    size = col.shape[0]
    spread = jnp.where(iota((size, LANES), 1) % size == iota((size, LANES), 0), col, 0.0)
    return jnp.sum(spread, axis=0, keepdims=True)


def decays(inv_col):
    modes = inv_col.shape[0]
    offset = iota((modes, LANES), 1).astype(F32)
    age_in = (LANES - offset) * inv_col
    age_out = offset * inv_col
    return jnp.exp(-age_in), age_in, jnp.exp(-age_out), age_out


def tile_modes(data):
    return jnp.concatenate([data] * (LANES // data.shape[0]), axis=0)


def is_early(seq_size):
    return lax.axis_index("seq") < seq_size // 2


def prepare(seq_size, memory_ref, residue_ref, skip_ref, x_ref, q_ref, k_ref, d_ref, table_ref, base_ref, read_ref):
    modes = memory_ref.shape[1]
    channels, local_len = x_ref.shape
    chunks = local_len // LANES
    rows = chunks * channels
    me_seq = lax.axis_index("seq")
    inv = 1.0 / memory_ref[...]
    inv_col = column(inv)
    inv_row = tiled_row(inv_col)
    decay_in, _, decay_out, _ = decays(inv_col)
    amplitude = column(residue_ref[...] * jnp.sqrt(2.0 * inv))
    values = by_chunk(x_ref) * by_chunk(k_ref)
    grads = by_chunk(d_ref) * by_chunk(q_ref)
    value_split = left_split(values)
    grad_split = left_split(grads)

    device = iota((seq_size, LANES), 0)
    ahead = (me_seq - 1 - device).astype(F32) * local_len
    behind = (device - me_seq - 1).astype(F32) * local_len
    table_ref[:seq_size] = jnp.where(ahead >= 0, jnp.exp(-jnp.maximum(ahead, 0.0) * inv_row), 0.0)
    table_ref[seq_size : 2 * seq_size] = jnp.where(behind >= 0, jnp.exp(-jnp.maximum(behind, 0.0) * inv_row), 0.0)
    power = iota((chunks, LANES), 0).astype(F32) * LANES
    table_ref[2 * seq_size : 2 * seq_size + chunks] = jnp.exp(-power * inv_row)

    read_in, read_out = tile_modes(amplitude * decay_in), tile_modes(amplitude * decay_out)
    read_ref[:LANES] = jnp.concatenate(halves(read_out), axis=1)
    read_ref[LANES:] = jnp.concatenate(halves(read_in), axis=1)

    value_states = contract(value_split, right_split(tile_modes(decay_in)), 1, 1)
    grad_states = contract(grad_split, right_split(tile_modes(decay_out)), 1, 1)
    step = jnp.exp(-LANES * inv_row)
    starts, ends = [jnp.zeros((channels, LANES), F32)], [jnp.zeros((channels, LANES), F32)]
    for j in range(chunks - 1):
        starts.append(step * starts[-1] + value_states[j * channels : (j + 1) * channels])
        i = chunks - 1 - j
        ends.append(step * ends[-1] + grad_states[i * channels : (i + 1) * channels])
    first = iota((rows, LANES), 1) < modes

    def state_split(parts):
        return left_split(jnp.where(first, jnp.concatenate(parts, axis=0), 0.0))

    taps = jnp.sum(amplitude * decay_out, axis=0, keepdims=True)
    square = (LANES, LANES)
    toeplitz = pltpu.roll(jnp.broadcast_to(taps, square), 0, 1, stride=1, stride_axis=0)
    toeplitz = jnp.where(iota(square, 1) >= iota(square, 0), toeplitz, 0.0)
    conv = contract(value_split, right_split(toeplitz, axis=0), 1, 0)
    conv = conv + contract(state_split(starts), right_split(read_out, axis=0), 1, 0)
    corr = contract(grad_split, right_split(toeplitz), 1, 1)
    corr = corr + contract(state_split(ends[::-1]), right_split(read_in, axis=0), 1, 0)
    gain = jnp.concatenate([column(skip_ref[...])] * chunks, axis=0)
    base_ref[:rows] = conv + gain * values
    base_ref[rows:] = corr + gain * grads


def make_states(seq_size, *refs):
    sources, (out_ref, *copies), tables, arrived = refs[:7], refs[7:15], refs[15:18], refs[18]
    moves = [pltpu.make_async_copy(*ends, arrived.at[i]) for i, ends in enumerate(zip(sources, copies))]
    for move in moves:
        move.start()
    memory_ref, _, _, x_ref, q_ref, k_ref, d_ref = copies
    modes = memory_ref.shape[1]
    channels, local_len = x_ref.shape
    chunks = local_len // LANES
    moves[0].wait()
    inv_col = column(1.0 / memory_ref[...])
    inv_row = tiled_row(inv_col)
    decay_in, age_in, decay_out, age_out = decays(inv_col)
    pair_in = jnp.concatenate([tile_modes(decay_in), tile_modes(decay_in * age_in)], axis=0)
    pair_out = jnp.concatenate([tile_modes(decay_out), tile_modes(decay_out * age_out)], axis=0)
    split_in, split_out = right_split(pair_in), right_split(pair_out)
    step = jnp.exp(-LANES * inv_row)
    growth = LANES * inv_row
    for move in moves[1:]:
        move.wait()
    values = by_chunk(x_ref) * by_chunk(k_ref)
    grads = by_chunk(d_ref) * by_chunk(q_ref)
    value_states = contract(left_split(values), split_in, 1, 1)
    grad_states = contract(left_split(grads), split_out, 1, 1)
    outer = contract(left_split(values, axis=0), right_split(grads, axis=0), 0, 0)
    outer = jnp.where(iota(outer.shape, 1) >= iota(outer.shape, 0), outer, 0.0)
    turn = (iota(outer.shape, 1) + iota(outer.shape, 0)) % LANES
    skewed = jnp.take_along_axis(outer, turn, axis=1, mode="promise_in_bounds")
    near = decay_out * jnp.sum(skewed, axis=0, keepdims=True)
    near_zero = jnp.sum(near, axis=1, keepdims=True)
    near_one = jnp.sum(near * age_out, axis=1, keepdims=True)
    products = values * grads
    part_skip = products[:channels]
    for j in range(1, chunks):
        part_skip = part_skip + products[j * channels : (j + 1) * channels]
    part_skip = jnp.sum(part_skip, axis=1, keepdims=True)
    lane = iota((channels, LANES), 1)
    row_id = iota((channels, LANES), 0)
    prefix_zero = jnp.zeros((channels, LANES), F32)
    prefix_one = cross_zero = cross_one = suffix_zero = suffix_one = prefix_zero
    power = jnp.ones_like(step)
    for j in range(chunks):
        rows = slice(j * channels, (j + 1) * channels)
        grad_zero, grad_one = grad_states[rows, :LANES], grad_states[rows, LANES:]
        if j > 0:
            cross_zero = cross_zero + prefix_zero * grad_zero
            cross_one = cross_one + prefix_one * grad_zero + prefix_zero * grad_one
        prefix_one = step * (prefix_one + growth * prefix_zero) + value_states[rows, LANES:]
        prefix_zero = step * prefix_zero + value_states[rows, :LANES]
        suffix_zero = suffix_zero + power * grad_zero
        suffix_one = suffix_one + power * (grad_one + j * growth * grad_zero)
        power = power * step
    half = channels // 2
    own = lane // modes == row_id % half
    for kind, state in enumerate((prefix_zero, prefix_one, suffix_zero, suffix_one)):
        state = jnp.where(own, state, 0.0)
        out_ref[2 * kind] = jnp.sum(state[:half], axis=0, keepdims=True)
        out_ref[2 * kind + 1] = jnp.sum(state[half:], axis=0, keepdims=True)
    extras = (
        jnp.where(lane < modes, cross_zero, 0.0)
        + jnp.where((lane >= modes) & (lane < 2 * modes), cross_one, 0.0)
        + jnp.where(lane == row_id, near_zero, 0.0)
        + jnp.where(lane == row_id + modes, near_one, 0.0)
        + jnp.where(lane == row_id + 2 * modes, part_skip, 0.0)
    )
    out_ref[8] = jnp.sum(extras, axis=0, keepdims=True)

    @pl.when(is_early(seq_size))
    def _():
        prepare(seq_size, *copies, *tables)


def finish(seq_size, ch_size, *refs):
    arguments, all_ref, early, refs = refs[:7], refs[7], refs[8:11], refs[11:]
    results, scratch, late, sent = refs[:7], refs[7:14], refs[14:17], refs[17]
    memory_ref, residue_ref, _, x_ref, q_ref, k_ref, d_ref = arguments
    grad_skip_ref, grad_residue_ref, grad_memory_ref = scratch[4:]
    moves = [pltpu.make_async_copy(*ends, sent.at[i]) for i, ends in enumerate(zip(scratch, results))]
    modes = memory_ref.shape[1]
    channels, local_len = x_ref.shape
    chunks = local_len // LANES
    half = channels // 2
    rows = chunks * channels
    block = 9

    def strided(start, count, stride):
        return all_ref[pl.ds(start, count, stride=stride), :]

    def outputs(table_ref, base_ref, read_ref):
        me = lax.axis_index("ch") * seq_size * block
        own = iota((half, LANES), 1) // modes == iota((half, LANES), 0)

        def border(kind, weights):
            parts = []
            for part in range(2):
                state = strided(me + 2 * kind + part, seq_size, block)
                state = jnp.sum(weights * state, axis=0, keepdims=True)
                parts.append(jnp.where(own, state, 0.0))
            return jnp.concatenate(parts, axis=0)

        before = border(0, table_ref[:seq_size])
        after = border(2, table_ref[seq_size : 2 * seq_size])
        powers = [table_ref[2 * seq_size + j : 2 * seq_size + j + 1] for j in range(chunks)]

        def readout(state, factors, matrix):
            high, low = halves(jnp.concatenate([factor * state for factor in factors], axis=0))
            product = contract(jnp.concatenate([high, low], axis=0), matrix, 1, 0)
            return product[:rows, :LANES] + product[:rows, LANES:] + product[rows:, :LANES]

        mixed = base_ref[:rows] + readout(before, powers, read_ref[:LANES])
        grad_values = base_ref[rows:] + readout(after, powers[::-1], read_ref[LANES:])
        for i, (gate_ref, data) in enumerate(
            ((q_ref, mixed), (k_ref, grad_values), (d_ref, mixed), (x_ref, grad_values))
        ):
            for j in range(chunks):
                lanes = slice(j * LANES, (j + 1) * LANES)
                part = gate_ref[:, lanes].astype(F32) * data[j * channels : (j + 1) * channels]
                scratch[i][:, lanes] = part.astype(BF16)
            moves[i].start()

    @pl.when(is_early(seq_size))
    def _():
        outputs(*early)

    @pl.when(jnp.logical_not(is_early(seq_size)))
    def _():
        prepare(seq_size, *arguments, *late)
        outputs(*late)

    inv = 1.0 / memory_ref[...]
    inv_row = tiled_row(column(inv))
    leap = jnp.exp(-local_len * inv_row)
    growth = local_len * inv_row

    def pairs(e, carry):
        done = []
        for part, (prefix_zero, prefix_one, cross_zero, cross_one) in enumerate(carry):
            value_zero, value_one, grad_zero, grad_one = [
                strided(e * block + 2 * kind + part, ch_size, seq_size * block) for kind in range(4)
            ]
            done.append(
                (
                    leap * prefix_zero + value_zero,
                    leap * (prefix_one + growth * prefix_zero) + value_one,
                    cross_zero + prefix_zero * grad_zero,
                    cross_one + prefix_one * grad_zero + prefix_zero * grad_one,
                )
            )
        return tuple(done)

    zeros = jnp.zeros((ch_size, LANES), F32)
    carry = ((zeros,) * 4,) * 2
    if seq_size <= 8:
        for e in range(seq_size):
            carry = pairs(e, carry)
    else:
        carry = lax.fori_loop(0, seq_size, pairs, carry)
    sums = [jnp.sum(carry[0][i] + carry[1][i], axis=0, keepdims=True) for i in (2, 3)]
    extras = jnp.sum(strided(8, ch_size * seq_size, block), axis=0, keepdims=True)
    kind = iota((8, LANES), 0)
    sums = jnp.where(kind == 0, sums[0], sums[1])
    shift = LANES // 2
    while shift >= modes:
        sums = sums + roll(sums, shift)
        shift //= 2
    sum_zero = sums[0:1, :modes] + extras[:, :modes]
    sum_one = sums[1:2, :modes] + roll(extras, -modes)[:, :modes]
    scale = jnp.sqrt(2.0 * inv) / math.sqrt(ch_size * channels * seq_size * local_len)
    grad_residue_ref[...] = scale * sum_zero
    grad_memory_ref[...] = residue_ref[...] * scale * (sum_one - 0.5 * sum_zero)
    skip = strided(lax.axis_index("ch") * seq_size * block + 8, seq_size, block)
    skip = roll(jnp.sum(skip, axis=0, keepdims=True), -2 * modes)
    grad_skip_ref[...] = skip[:, :channels] / math.sqrt(seq_size * local_len)
    for move in moves[4:]:
        move.start()
    for move in moves:
        move.wait()


def per_device(signal_x, gate_q, gate_k, skip_gain, residue, memory, cotangent):
    channels, local_len = signal_x.shape
    modes = memory.shape[0]
    seq_size, ch_size = lax.axis_size("seq"), lax.axis_size("ch")
    devices = seq_size * ch_size
    params = pltpu.CompilerParams(vmem_limit_bytes=32 * 1024 * 1024)
    in_hbm = pl.BlockSpec(memory_space=pltpu.HBM)
    arguments = (memory[None], residue[None], skip_gain[None], signal_x, gate_q, gate_k, cotangent)
    arguments = [pltpu.with_memory_space_constraint(data, pltpu.HBM) for data in arguments]
    copies = [(data.shape, data.dtype) for data in arguments]
    rows = local_len // LANES * channels
    tables = [((2 * seq_size + 8, LANES), F32), ((2 * rows, LANES), F32), ((2 * LANES, 2 * LANES), BF16)]
    mine, *rest = pl.pallas_call(
        functools.partial(make_states, seq_size),
        in_specs=[in_hbm] * 7,
        out_shape=[jax.ShapeDtypeStruct(*shape) for shape in [((9, 1, LANES), F32), *copies, *tables]],
        scratch_shapes=[pltpu.SemaphoreType.DMA((7,))],
        compiler_params=params,
    )(*arguments)
    everyone = lax.all_to_all(jnp.broadcast_to(mine[None], (devices, 9, 1, LANES)), AXES, 0, 0)
    big = ((channels, local_len), BF16)
    shapes = [big] * 4 + [((1, channels), F32), ((1, modes), F32), ((1, modes), F32)]
    results = pl.pallas_call(
        functools.partial(finish, seq_size, ch_size),
        out_shape=[jax.ShapeDtypeStruct(*shape) for shape in shapes],
        out_specs=[in_hbm] * 7,
        scratch_shapes=[*[pltpu.VMEM(*shape) for shape in shapes + tables], pltpu.SemaphoreType.DMA((7,))],
        compiler_params=params,
    )(*rest[:7], everyone.reshape(devices * 9, LANES), *rest[7:])
    return (*results[:4], *[result[0] for result in results[4:]])


def solution(mesh):
    grid = P("ch", "seq")
    return jax.shard_map(
        per_device,
        mesh=mesh,
        in_specs=(grid, grid, grid, P("ch"), P(), P(), grid),
        out_specs=(grid, grid, grid, grid, P("ch"), P(), P()),
        check_vma=False,
    )
```

time: 19.1 us -> 18.4 us (0.963)
  blocking collectives: 15.5 us -> 14.4 us
  Pallas kernels: 2.64 us -> 2.95 us
    all_to_all x1, blocking collectives: 15.5 us -> 14.4 us  [per_device(): lax.all_to_all(jnp.broadcast_to(mine[None], (devices, 9, 1, LANES)), AXES...]
    pallas_call x1, Pallas kernels: 1.4 us -> 1.85 us  [per_device(): pl.pallas_call(functools.partial(make_states, seq_size), in_specs=[in_hbm...]
where the time goes in v1:
time: 18.4 us; the launch traced here: 18.1 us
  blocking collectives  14.4 us (78%)
  Pallas kernels  2.95 us (16%)
  between operations  0.66 us (4%)
    all_to_all x1, blocking collectives, per_device(): lax.all_to_all(jnp.broadcast_to(mine[None], (devices, 9, 1, LANES)), AXES...  14.4 us
    pallas_call x1, Pallas kernels, per_device(): pl.pallas_call(functools.partial(make_states, seq_size), in_specs=[in_hbm...  1.85 us
    pallas_call x1, Pallas kernels, per_device(): pl.pallas_call(functools.partial(finish, seq_size, ch_size), out_shape=[j...  1.11 us

profile of v1, /device:TPU:0, one launch (start us, length us, event | category | flops | bytes accessed | tf_op | source)
XLA Modules:
  0.0 18.1 jit_solution(2208969495530104080)
XLA Ops:
  0.6 1.8 %shard_map.126 = (f32[9,1,128]{2,1,0:T(1,128)S(1)}, f32[1,16]{1,0:T(1,128)S(1)}, f32[1,16]{1,0:T(1,128)S(1)}, f32[1,16]{1,0:T(1,128)S(1)}, bf16[16,512]{1,0:T(8,...) custom-call(f32[1,16]{1,0:T(1,128)} %bitcast.12, ...), custom_call_target="tpu_custom_call" | custom-call | tf_op jit(solution)/shard_map/pallas_call | solution.py:323
  2.5 0.1 broadcast_in_dim.21
  2.6 14.4 %all_to_all.5 = f32[32,9,1,128]{3,2,1,0:T(1,128)S(1)} all-to-all(f32[32,9,1,128]{3,2,1,0:T(1,128)S(1)} %broadcast_in_dim.21), channel_id=1, replica_groups=mesh['seq'=8,'ch'=4] {'ch','seq'}, dimensions={0} | all-to-all | bytes 294912 | tf_op jit(solution)/shard_map/all_to_all | solution.py:330
  17.0 1.1 %shard_map.127 = (bf16[16,512]{1,0:T(8,128)(2,1)}, bf16[16,512]{1,0:T(8,128)(2,1)}, bf16[16,512]{1,0:T(8,128)(2,1)}, bf16[16,512]{1,0:T(8,128)(2,1)}, f32[1,16]{...) custom-call(f32[1,16]{1,0:T(1,128)S(1)} %get-tuple-element.25.refs_0_, f32[1,16]{1,0:T(1,128)S(1)} %get-tuple-element.26.refs_1_, ...), custom_call_target="tpu_custom_call" | custom-call | tf_op jit(solution)/shard_map/pallas_call | solution.py:333
  (1 shorter events, 0.0 us)

commit v2 on v1

--- a/solution.py
+++ b/solution.py
@@ -132,8 +132,8 @@
 def make_states(seq_size, *refs):
     sources, (out_ref, *copies), tables, arrived = refs[:7], refs[7:15], refs[15:18], refs[18]
     moves = [pltpu.make_async_copy(*ends, arrived.at[i]) for i, ends in enumerate(zip(sources, copies))]
-    for move in moves:
-        move.start()
+    for i in (0, 3, 5, 6, 4, 1, 2):
+        moves[i].start()
     memory_ref, _, _, x_ref, q_ref, k_ref, d_ref = copies
     modes = memory_ref.shape[1]
     channels, local_len = x_ref.shape
@@ -147,7 +147,7 @@
     split_in, split_out = right_split(pair_in), right_split(pair_out)
     step = jnp.exp(-LANES * inv_row)
     growth = LANES * inv_row
-    for move in moves[1:]:
+    for move in moves[3:]:
         move.wait()
     values = by_chunk(x_ref) * by_chunk(k_ref)
     grads = by_chunk(d_ref) * by_chunk(q_ref)
@@ -183,10 +183,11 @@
         power = power * step
     half = channels // 2
     own = lane // modes == row_id % half
-    for kind, state in enumerate((prefix_zero, prefix_one, suffix_zero, suffix_one)):
+    payload = []
+    for state in (prefix_zero, prefix_one, suffix_zero, suffix_one):
         state = jnp.where(own, state, 0.0)
-        out_ref[2 * kind] = jnp.sum(state[:half], axis=0, keepdims=True)
-        out_ref[2 * kind + 1] = jnp.sum(state[half:], axis=0, keepdims=True)
+        payload.append(jnp.sum(state[:half], axis=0, keepdims=True))
+        payload.append(jnp.sum(state[half:], axis=0, keepdims=True))
     extras = (
         jnp.where(lane < modes, cross_zero, 0.0)
         + jnp.where((lane >= modes) & (lane < 2 * modes), cross_one, 0.0)
@@ -194,7 +195,17 @@
         + jnp.where(lane == row_id + modes, near_one, 0.0)
         + jnp.where(lane == row_id + 2 * modes, part_skip, 0.0)
     )
-    out_ref[8] = jnp.sum(extras, axis=0, keepdims=True)
+    payload.append(jnp.sum(extras, axis=0, keepdims=True))
+    sublane = iota((8, LANES), 0)
+    for k in range(len(payload)):
+        tile = jnp.zeros((8, LANES), F32)
+        for i in range(8):
+            tile = jnp.where(sublane == i, payload[(8 * k + i) % len(payload)], tile)
+        for start in range(8 * k, out_ref.shape[0], 8 * len(payload)):
+            out_ref[start : start + 8] = tile
+
+    for move in moves[1:3]:
+        move.wait()
 
     @pl.when(is_early(seq_size))
     def _():
@@ -217,7 +228,7 @@
     def strided(start, count, stride):
         return all_ref[pl.ds(start, count, stride=stride), :]
 
-    def outputs(table_ref, base_ref, read_ref):
+    def complete(table_ref, base_ref, read_ref):
         me = lax.axis_index("ch") * seq_size * block
         own = iota((half, LANES), 1) // modes == iota((half, LANES), 0)
 
@@ -240,6 +251,49 @@
 
         mixed = base_ref[:rows] + readout(before, powers, read_ref[:LANES])
         grad_values = base_ref[rows:] + readout(after, powers[::-1], read_ref[LANES:])
+
+        inv = 1.0 / memory_ref[...]
+        inv_row = tiled_row(column(inv))
+        leap = jnp.exp(-local_len * inv_row)
+        growth = local_len * inv_row
+
+        def pairs(e, carry):
+            done = []
+            for part, (prefix_zero, prefix_one, cross_zero, cross_one) in enumerate(carry):
+                value_zero, value_one, grad_zero, grad_one = [
+                    strided(e * block + 2 * kind + part, ch_size, seq_size * block) for kind in range(4)
+                ]
+                done.append(
+                    (
+                        leap * prefix_zero + value_zero,
+                        leap * (prefix_one + growth * prefix_zero) + value_one,
+                        cross_zero + prefix_zero * grad_zero,
+                        cross_one + prefix_one * grad_zero + prefix_zero * grad_one,
+                    )
+                )
+            return tuple(done)
+
+        zeros = jnp.zeros((ch_size, LANES), F32)
+        carry = ((zeros,) * 4,) * 2
+        if seq_size <= 8:
+            for e in range(seq_size):
+                carry = pairs(e, carry)
+        else:
+            carry = lax.fori_loop(0, seq_size, pairs, carry)
+        sums = [jnp.sum(carry[0][i] + carry[1][i], axis=0, keepdims=True) for i in (2, 3)]
+        extras = jnp.sum(strided(8, ch_size * seq_size, block), axis=0, keepdims=True)
+        kind = iota((8, LANES), 0)
+        sums = jnp.where(kind == 0, sums[0], sums[1])
+        shift = LANES // 2
+        while shift >= modes:
+            sums = sums + roll(sums, shift)
+            shift //= 2
+        sum_zero = sums[0:1, :modes] + extras[:, :modes]
+        sum_one = sums[1:2, :modes] + roll(extras, -modes)[:, :modes]
+        scale = jnp.sqrt(2.0 * inv) / math.sqrt(ch_size * channels * seq_size * local_len)
+        skip = jnp.sum(strided(me + 8, seq_size, block), axis=0, keepdims=True)
+        skip = roll(skip, -2 * modes)[:, :channels] / math.sqrt(seq_size * local_len)
+
         for i, (gate_ref, data) in enumerate(
             ((q_ref, mixed), (k_ref, grad_values), (d_ref, mixed), (x_ref, grad_values))
         ):
@@ -247,63 +301,21 @@
                 lanes = slice(j * LANES, (j + 1) * LANES)
                 part = gate_ref[:, lanes].astype(F32) * data[j * channels : (j + 1) * channels]
                 scratch[i][:, lanes] = part.astype(BF16)
-            moves[i].start()
+        grad_skip_ref[...] = skip
+        grad_residue_ref[...] = scale * sum_zero
+        grad_memory_ref[...] = residue_ref[...] * scale * (sum_one - 0.5 * sum_zero)
+        for move in moves:
+            move.start()
 
     @pl.when(is_early(seq_size))
     def _():
-        outputs(*early)
+        complete(*early)
 
     @pl.when(jnp.logical_not(is_early(seq_size)))
     def _():
         prepare(seq_size, *arguments, *late)
-        outputs(*late)
-
-    inv = 1.0 / memory_ref[...]
-    inv_row = tiled_row(column(inv))
-    leap = jnp.exp(-local_len * inv_row)
-    growth = local_len * inv_row
-
-    def pairs(e, carry):
-        done = []
-        for part, (prefix_zero, prefix_one, cross_zero, cross_one) in enumerate(carry):
-            value_zero, value_one, grad_zero, grad_one = [
-                strided(e * block + 2 * kind + part, ch_size, seq_size * block) for kind in range(4)
-            ]
-            done.append(
-                (
-                    leap * prefix_zero + value_zero,
-                    leap * (prefix_one + growth * prefix_zero) + value_one,
-                    cross_zero + prefix_zero * grad_zero,
-                    cross_one + prefix_one * grad_zero + prefix_zero * grad_one,
-                )
-            )
-        return tuple(done)
-
-    zeros = jnp.zeros((ch_size, LANES), F32)
-    carry = ((zeros,) * 4,) * 2
-    if seq_size <= 8:
-        for e in range(seq_size):
-            carry = pairs(e, carry)
-    else:
-        carry = lax.fori_loop(0, seq_size, pairs, carry)
-    sums = [jnp.sum(carry[0][i] + carry[1][i], axis=0, keepdims=True) for i in (2, 3)]
-    extras = jnp.sum(strided(8, ch_size * seq_size, block), axis=0, keepdims=True)
-    kind = iota((8, LANES), 0)
-    sums = jnp.where(kind == 0, sums[0], sums[1])
-    shift = LANES // 2
-    while shift >= modes:
-        sums = sums + roll(sums, shift)
-        shift //= 2
-    sum_zero = sums[0:1, :modes] + extras[:, :modes]
-    sum_one = sums[1:2, :modes] + roll(extras, -modes)[:, :modes]
-    scale = jnp.sqrt(2.0 * inv) / math.sqrt(ch_size * channels * seq_size * local_len)
-    grad_residue_ref[...] = scale * sum_zero
-    grad_memory_ref[...] = residue_ref[...] * scale * (sum_one - 0.5 * sum_zero)
-    skip = strided(lax.axis_index("ch") * seq_size * block + 8, seq_size, block)
-    skip = roll(jnp.sum(skip, axis=0, keepdims=True), -2 * modes)
-    grad_skip_ref[...] = skip[:, :channels] / math.sqrt(seq_size * local_len)
-    for move in moves[4:]:
-        move.start()
+        complete(*late)
+
     for move in moves:
         move.wait()
 
@@ -323,11 +335,11 @@
     mine, *rest = pl.pallas_call(
         functools.partial(make_states, seq_size),
         in_specs=[in_hbm] * 7,
-        out_shape=[jax.ShapeDtypeStruct(*shape) for shape in [((9, 1, LANES), F32), *copies, *tables]],
+        out_shape=[jax.ShapeDtypeStruct(*shape) for shape in [((devices * 9, LANES), F32), *copies, *tables]],
         scratch_shapes=[pltpu.SemaphoreType.DMA((7,))],
         compiler_params=params,
     )(*arguments)
-    everyone = lax.all_to_all(jnp.broadcast_to(mine[None], (devices, 9, 1, LANES)), AXES, 0, 0)
+    everyone = lax.all_to_all(mine.reshape(devices, 9, 1, LANES), AXES, 0, 0)
     big = ((channels, local_len), BF16)
     shapes = [big] * 4 + [((1, channels), F32), ((1, modes), F32), ((1, modes), F32)]
     results = pl.pallas_call(

time: 18.4 us -> 18.1 us (0.984)
  no operation moved by 1% of the time
where the time goes in v2:
time: 18.1 us; the launch traced here: 17.9 us
  blocking collectives  14.4 us (80%)
  Pallas kernels  2.8 us (15%)
  between operations  0.64 us (4%)
    all_to_all x1, blocking collectives, per_device(): everyone = lax.all_to_all(mine.reshape(devices, 9, 1, LANES), AXES, 0, 0)  14.4 us
    pallas_call x1, Pallas kernels, per_device(): pl.pallas_call(functools.partial(make_states, seq_size), in_specs=[in_hbm...  1.86 us
    pallas_call x1, Pallas kernels, per_device(): pl.pallas_call(functools.partial(finish, seq_size, ch_size), out_shape=[j...  0.95 us

profile of v2, /device:TPU:0, one launch (start us, length us, event | category | flops | bytes accessed | tf_op | source)
XLA Modules:
  0.0 17.9 jit_solution(14767043353009821905)
XLA Ops:
  0.6 1.9 %shard_map.126 = (f32[288,128]{1,0:T(8,128)S(1)}, f32[1,16]{1,0:T(1,128)S(1)}, f32[1,16]{1,0:T(1,128)S(1)}, f32[1,16]{1,0:T(1,128)S(1)}, bf16[16,512]{1,0:T(8,12...) custom-call(f32[1,16]{1,0:T(1,128)} %bitcast.10, ...), custom_call_target="tpu_custom_call" | custom-call | tf_op jit(solution)/shard_map/pallas_call | solution.py:335
  2.5 14.4 %all_to_all.5 = f32[32,9,1,128]{3,2,1,0:T(1,128)S(1)} all-to-all(f32[32,9,1,128]{3,2,1,0:T(1,128)S(1)} %bitcast.9), channel_id=1, replica_groups=mesh['seq'=8,'ch'=4] {'ch','seq'}, dimensions={0} | all-to-all | bytes 294912 | tf_op jit(solution)/shard_map/all_to_all | solution.py:342
  16.9 0.9 %shard_map.127 = (bf16[16,512]{1,0:T(8,128)(2,1)}, bf16[16,512]{1,0:T(8,128)(2,1)}, bf16[16,512]{1,0:T(8,128)(2,1)}, bf16[16,512]{1,0:T(8,128)(2,1)}, f32[1,16]{...) custom-call(f32[1,16]{1,0:T(1,128)S(1)} %get-tuple-element.25.refs_0_, f32[1,16]{1,0:T(1,128)S(1)} %get-tuple-element.26.refs_1_, ...), custom_call_target="tpu_custom_call" | custom-call | tf_op jit(solution)/shard_map/pallas_call | solution.py:345

commit v3 on v2

--- a/solution.py
+++ b/solution.py
@@ -11,7 +11,7 @@
 F32 = jnp.float32
 BF16 = jnp.bfloat16
 LANES = 128
-AXES = ("ch", "seq")
+AXES = ("seq", "ch")
 
 
 def iota(shape, dim):
@@ -69,6 +69,18 @@
 
 def tile_modes(data):
     return jnp.concatenate([data] * (LANES // data.shape[0]), axis=0)
+
+
+def ranks(size, tuned):
+    return tuned if len(tuned) == size else tuple(range(size))
+
+
+def seq_ranks(seq_size):
+    return ranks(seq_size, (6, 0, 2, 7, 4, 5, 3, 1))
+
+
+def ch_ranks(ch_size):
+    return ranks(ch_size, (2, 0, 3, 1))
 
 
 def is_early(seq_size):
@@ -92,12 +104,19 @@
     grad_split = left_split(grads)
 
     device = iota((seq_size, LANES), 0)
+    if seq_ranks(seq_size) != tuple(range(seq_size)):
+        place = device
+        for p, index in enumerate(seq_ranks(seq_size)):
+            device = jnp.where(place == p, index, device)
     ahead = (me_seq - 1 - device).astype(F32) * local_len
     behind = (device - me_seq - 1).astype(F32) * local_len
     table_ref[:seq_size] = jnp.where(ahead >= 0, jnp.exp(-jnp.maximum(ahead, 0.0) * inv_row), 0.0)
     table_ref[seq_size : 2 * seq_size] = jnp.where(behind >= 0, jnp.exp(-jnp.maximum(behind, 0.0) * inv_row), 0.0)
     power = iota((chunks, LANES), 0).astype(F32) * LANES
     table_ref[2 * seq_size : 2 * seq_size + chunks] = jnp.exp(-power * inv_row)
+    leap = jnp.exp(-local_len * inv_row)
+    table_ref[2 * seq_size + chunks : 2 * seq_size + chunks + 1] = leap
+    table_ref[2 * seq_size + chunks + 1 : 2 * seq_size + chunks + 2] = leap * (local_len * inv_row)
 
     read_in, read_out = tile_modes(amplitude * decay_in), tile_modes(amplitude * decay_out)
     read_ref[:LANES] = jnp.concatenate(halves(read_out), axis=1)
@@ -147,12 +166,12 @@
     split_in, split_out = right_split(pair_in), right_split(pair_out)
     step = jnp.exp(-LANES * inv_row)
     growth = LANES * inv_row
-    for move in moves[3:]:
-        move.wait()
+    moves[3].wait()
+    moves[5].wait()
     values = by_chunk(x_ref) * by_chunk(k_ref)
+    moves[6].wait()
+    moves[4].wait()
     grads = by_chunk(d_ref) * by_chunk(q_ref)
-    value_states = contract(left_split(values), split_in, 1, 1)
-    grad_states = contract(left_split(grads), split_out, 1, 1)
     outer = contract(left_split(values, axis=0), right_split(grads, axis=0), 0, 0)
     outer = jnp.where(iota(outer.shape, 1) >= iota(outer.shape, 0), outer, 0.0)
     turn = (iota(outer.shape, 1) + iota(outer.shape, 0)) % LANES
@@ -160,6 +179,8 @@
     near = decay_out * jnp.sum(skewed, axis=0, keepdims=True)
     near_zero = jnp.sum(near, axis=1, keepdims=True)
     near_one = jnp.sum(near * age_out, axis=1, keepdims=True)
+    value_states = contract(left_split(values), split_in, 1, 1)
+    grad_states = contract(left_split(grads), split_out, 1, 1)
     products = values * grads
     part_skip = products[:channels]
     for j in range(1, chunks):
@@ -229,7 +250,9 @@
         return all_ref[pl.ds(start, count, stride=stride), :]
 
     def complete(table_ref, base_ref, read_ref):
-        me = lax.axis_index("ch") * seq_size * block
+        me = 0
+        for p, index in enumerate(ch_ranks(ch_size)):
+            me = me + jnp.where(lax.axis_index("ch") == index, p * seq_size * block, 0)
         own = iota((half, LANES), 1) // modes == iota((half, LANES), 0)
 
         def border(kind, weights):
@@ -253,9 +276,8 @@
         grad_values = base_ref[rows:] + readout(after, powers[::-1], read_ref[LANES:])
 
         inv = 1.0 / memory_ref[...]
-        inv_row = tiled_row(column(inv))
-        leap = jnp.exp(-local_len * inv_row)
-        growth = local_len * inv_row
+        at = 2 * seq_size + chunks
+        leap, leap_growth = table_ref[at : at + 1], table_ref[at + 1 : at + 2]
 
         def pairs(e, carry):
             done = []
@@ -266,7 +288,7 @@
                 done.append(
                     (
                         leap * prefix_zero + value_zero,
-                        leap * (prefix_one + growth * prefix_zero) + value_one,
+                        leap * prefix_one + (leap_growth * prefix_zero + value_one),
                         cross_zero + prefix_zero * grad_zero,
                         cross_one + prefix_one * grad_zero + prefix_zero * grad_one,
                     )
@@ -275,9 +297,9 @@
 
         zeros = jnp.zeros((ch_size, LANES), F32)
         carry = ((zeros,) * 4,) * 2
-        if seq_size <= 8:
+        if seq_size <= 8 or seq_ranks(seq_size) != tuple(range(seq_size)):
             for e in range(seq_size):
-                carry = pairs(e, carry)
+                carry = pairs(seq_ranks(seq_size).index(e), carry)
         else:
             carry = lax.fori_loop(0, seq_size, pairs, carry)
         sums = [jnp.sum(carry[0][i] + carry[1][i], axis=0, keepdims=True) for i in (2, 3)]
@@ -339,7 +361,8 @@
         scratch_shapes=[pltpu.SemaphoreType.DMA((7,))],
         compiler_params=params,
     )(*arguments)
-    everyone = lax.all_to_all(mine.reshape(devices, 9, 1, LANES), AXES, 0, 0)
+    order = [s * ch_size + c for c in ch_ranks(ch_size) for s in seq_ranks(seq_size)]
+    everyone = lax.all_to_all(mine.reshape(devices, 9, 1, LANES), AXES, 0, 0, axis_index_groups=[order])
     big = ((channels, local_len), BF16)
     shapes = [big] * 4 + [((1, channels), F32), ((1, modes), F32), ((1, modes), F32)]
     results = pl.pallas_call(

time: 18.1 us -> 17.3 us (0.956)
  blocking collectives: 14.4 us -> 13.8 us
    all_to_all x1, blocking collectives: 14.4 us -> 13.8 us  [per_device(): lax.all_to_all(mine.reshape(devices, 9, 1, LANES), AXES, 0, 0, axis_index...]
where the time goes in v3:
time: 17.3 us; the launch traced here: 17.1 us
  blocking collectives  13.8 us (80%)
  Pallas kernels  2.64 us (15%)
  between operations  0.64 us (4%)
    all_to_all x1, blocking collectives, per_device(): lax.all_to_all(mine.reshape(devices, 9, 1, LANES), AXES, 0, 0, axis_index...  13.8 us
    pallas_call x1, Pallas kernels, per_device(): pl.pallas_call(functools.partial(make_states, seq_size), in_specs=[in_hbm...  1.76 us
    pallas_call x1, Pallas kernels, per_device(): pl.pallas_call(functools.partial(finish, seq_size, ch_size), out_shape=[j...  0.88 us

profile of v3, /device:TPU:0, one launch (start us, length us, event | category | flops | bytes accessed | tf_op | source)
XLA Modules:
  0.0 17.1 jit_solution(5629239797320862805)
XLA Ops:
  0.6 1.8 %shard_map.126 = (f32[288,128]{1,0:T(8,128)S(1)}, f32[1,16]{1,0:T(1,128)S(1)}, f32[1,16]{1,0:T(1,128)S(1)}, f32[1,16]{1,0:T(1,128)S(1)}, bf16[16,512]{1,0:T(8,12...) custom-call(f32[1,16]{1,0:T(1,128)} %bitcast.10, ...), custom_call_target="tpu_custom_call" | custom-call | tf_op jit(solution)/shard_map/pallas_call | solution.py:357
  2.4 13.8 %all_to_all.5 = f32[32,9,1,128]{3,2,1,0:T(1,128)S(1)} all-to-all(f32[32,9,1,128]{3,2,1,0:T(1,128)S(1)} %bitcast.9), channel_id=1, replica_groups={{26,2,10,30,18,22,14,6,24,0,8,28,16,20,12,4,27,3,11,31,19,23,15,7,25,1,..., dimensions={0} | all-to-all | bytes 294912 | tf_op jit(solution)/shard_map/all_to_all | solution.py:365
  16.2 0.9 %shard_map.127 = (bf16[16,512]{1,0:T(8,128)(2,1)}, bf16[16,512]{1,0:T(8,128)(2,1)}, bf16[16,512]{1,0:T(8,128)(2,1)}, bf16[16,512]{1,0:T(8,128)(2,1)}, f32[1,16]{...) custom-call(f32[1,16]{1,0:T(1,128)S(1)} %get-tuple-element.25.refs_0_, f32[1,16]{1,0:T(1,128)S(1)} %get-tuple-element.26.refs_1_, ...), custom_call_target="tpu_custom_call" | custom-call | tf_op jit(solution)/shard_map/pallas_call | solution.py:368

commit v4 on v3

--- a/solution.py
+++ b/solution.py
@@ -12,6 +12,8 @@
 BF16 = jnp.bfloat16
 LANES = 128
 AXES = ("seq", "ch")
+CORES = 2
+BLOCK = 9
 
 
 def iota(shape, dim):
@@ -76,15 +78,19 @@
 
 
 def seq_ranks(seq_size):
-    return ranks(seq_size, (6, 0, 2, 7, 4, 5, 3, 1))
-
-
-def ch_ranks(ch_size):
-    return ranks(ch_size, (2, 0, 3, 1))
-
-
-def is_early(seq_size):
-    return lax.axis_index("seq") < seq_size // 2
+    return ranks(seq_size, (7, 0, 1, 4, 6, 3, 2, 5))
+
+
+def chip_ranks(chips):
+    return ranks(chips, (1, 0))
+
+
+def is_early():
+    return (lax.axis_index("seq") == 0) & (lax.axis_index("ch") < CORES)
+
+
+def strided(ref, start, count, stride):
+    return ref[pl.ds(start, count, stride=stride), :]
 
 
 def prepare(seq_size, memory_ref, residue_ref, skip_ref, x_ref, q_ref, k_ref, d_ref, table_ref, base_ref, read_ref):
@@ -114,9 +120,6 @@
     table_ref[seq_size : 2 * seq_size] = jnp.where(behind >= 0, jnp.exp(-jnp.maximum(behind, 0.0) * inv_row), 0.0)
     power = iota((chunks, LANES), 0).astype(F32) * LANES
     table_ref[2 * seq_size : 2 * seq_size + chunks] = jnp.exp(-power * inv_row)
-    leap = jnp.exp(-local_len * inv_row)
-    table_ref[2 * seq_size + chunks : 2 * seq_size + chunks + 1] = leap
-    table_ref[2 * seq_size + chunks + 1 : 2 * seq_size + chunks + 2] = leap * (local_len * inv_row)
 
     read_in, read_out = tile_modes(amplitude * decay_in), tile_modes(amplitude * decay_out)
     read_ref[:LANES] = jnp.concatenate(halves(read_out), axis=1)
@@ -149,7 +152,7 @@
 
 
 def make_states(seq_size, *refs):
-    sources, (out_ref, *copies), tables, arrived = refs[:7], refs[7:15], refs[15:18], refs[18]
+    sources, (out_ref, rates_ref, *copies), tables, arrived = refs[:7], refs[7:16], refs[16:19], refs[19]
     moves = [pltpu.make_async_copy(*ends, arrived.at[i]) for i, ends in enumerate(zip(sources, copies))]
     for i in (0, 3, 5, 6, 4, 1, 2):
         moves[i].start()
@@ -166,6 +169,9 @@
     split_in, split_out = right_split(pair_in), right_split(pair_out)
     step = jnp.exp(-LANES * inv_row)
     growth = LANES * inv_row
+    leap = jnp.exp(-local_len * inv_row)
+    rates_ref[0:1] = leap
+    rates_ref[1:2] = leap * (local_len * inv_row)
     moves[3].wait()
     moves[5].wait()
     values = by_chunk(x_ref) * by_chunk(k_ref)
@@ -228,37 +234,85 @@
     for move in moves[1:3]:
         move.wait()
 
-    @pl.when(is_early(seq_size))
+    @pl.when(is_early())
     def _():
         prepare(seq_size, *copies, *tables)
 
 
+def pair_sums(seq_size, chips, rates_ref, all_ref, sums_ref):
+    modes = LANES // 8
+    leap, leap_growth = rates_ref[0:1], rates_ref[1:2]
+
+    def pairs(e, carry):
+        done = []
+        for part, (prefix_zero, prefix_one, cross_zero, cross_one) in enumerate(carry):
+            value_zero, value_one, grad_zero, grad_one = [
+                strided(all_ref, e * BLOCK + 2 * kind + part, chips, seq_size * BLOCK) for kind in range(4)
+            ]
+            done.append(
+                (
+                    leap * prefix_zero + value_zero,
+                    leap * prefix_one + (leap_growth * prefix_zero + value_one),
+                    cross_zero + prefix_zero * grad_zero,
+                    cross_one + prefix_one * grad_zero + prefix_zero * grad_one,
+                )
+            )
+        return tuple(done)
+
+    zeros = jnp.zeros((chips, LANES), F32)
+    carry = ((zeros,) * 4,) * 2
+    if seq_size <= 8 or seq_ranks(seq_size) != tuple(range(seq_size)):
+        for e in range(seq_size):
+            carry = pairs(seq_ranks(seq_size).index(e), carry)
+    else:
+        carry = lax.fori_loop(0, seq_size, pairs, carry)
+    sums = [jnp.sum(carry[0][i] + carry[1][i], axis=0, keepdims=True) for i in (2, 3)]
+    extras = jnp.sum(strided(all_ref, BLOCK - 1, chips * seq_size, BLOCK), axis=0, keepdims=True)
+    sums = jnp.where(iota((8, LANES), 0) == 0, sums[0], sums[1])
+    shift = LANES // 2
+    while shift >= modes:
+        sums = sums + roll(sums, shift)
+        shift //= 2
+    lane = iota((1, LANES), 1)
+    sums_ref[...] = extras + jnp.where(lane < modes, sums[0:1], jnp.where(lane < 2 * modes, sums[1:2], 0.0))
+
+
+def filter_grads(total, memory_ref, residue_ref, mine_ref, other_ref, *refs):
+    results, scratch, sent = refs[:2], refs[2:4], refs[4]
+    modes = memory_ref.shape[1]
+    scale = jnp.sqrt(2.0 / memory_ref[...]) / math.sqrt(total)
+    sums = mine_ref[...] + other_ref[...]
+    sum_zero, sum_one = sums[:, :modes], roll(sums, -modes)[:, :modes]
+    scratch[0][...] = scale * sum_zero
+    scratch[1][...] = residue_ref[...] * scale * (sum_one - 0.5 * sum_zero)
+    moves = [pltpu.make_async_copy(*ends, sent.at[i]) for i, ends in enumerate(zip(scratch, results))]
+    for move in moves:
+        move.start()
+    for move in moves:
+        move.wait()
+
+
 def finish(seq_size, ch_size, *refs):
     arguments, all_ref, early, refs = refs[:7], refs[7], refs[8:11], refs[11:]
-    results, scratch, late, sent = refs[:7], refs[7:14], refs[14:17], refs[17]
-    memory_ref, residue_ref, _, x_ref, q_ref, k_ref, d_ref = arguments
-    grad_skip_ref, grad_residue_ref, grad_memory_ref = scratch[4:]
+    results, scratch, late, sent = refs[:5], refs[5:10], refs[10:13], refs[13]
+    _, _, _, x_ref, q_ref, k_ref, d_ref = arguments
     moves = [pltpu.make_async_copy(*ends, sent.at[i]) for i, ends in enumerate(zip(scratch, results))]
-    modes = memory_ref.shape[1]
     channels, local_len = x_ref.shape
+    modes = LANES // 8
     chunks = local_len // LANES
     half = channels // 2
     rows = chunks * channels
-    block = 9
-
-    def strided(start, count, stride):
-        return all_ref[pl.ds(start, count, stride=stride), :]
 
     def complete(table_ref, base_ref, read_ref):
         me = 0
-        for p, index in enumerate(ch_ranks(ch_size)):
-            me = me + jnp.where(lax.axis_index("ch") == index, p * seq_size * block, 0)
+        for p, index in enumerate(chip_ranks(ch_size // CORES)):
+            me = me + jnp.where(lax.axis_index("ch") // CORES == index, p * seq_size * BLOCK, 0)
         own = iota((half, LANES), 1) // modes == iota((half, LANES), 0)
 
         def border(kind, weights):
             parts = []
             for part in range(2):
-                state = strided(me + 2 * kind + part, seq_size, block)
+                state = strided(all_ref, me + 2 * kind + part, seq_size, BLOCK)
                 state = jnp.sum(weights * state, axis=0, keepdims=True)
                 parts.append(jnp.where(own, state, 0.0))
             return jnp.concatenate(parts, axis=0)
@@ -275,47 +329,8 @@
         mixed = base_ref[:rows] + readout(before, powers, read_ref[:LANES])
         grad_values = base_ref[rows:] + readout(after, powers[::-1], read_ref[LANES:])
 
-        inv = 1.0 / memory_ref[...]
-        at = 2 * seq_size + chunks
-        leap, leap_growth = table_ref[at : at + 1], table_ref[at + 1 : at + 2]
-
-        def pairs(e, carry):
-            done = []
-            for part, (prefix_zero, prefix_one, cross_zero, cross_one) in enumerate(carry):
-                value_zero, value_one, grad_zero, grad_one = [
-                    strided(e * block + 2 * kind + part, ch_size, seq_size * block) for kind in range(4)
-                ]
-                done.append(
-                    (
-                        leap * prefix_zero + value_zero,
-                        leap * prefix_one + (leap_growth * prefix_zero + value_one),
-                        cross_zero + prefix_zero * grad_zero,
-                        cross_one + prefix_one * grad_zero + prefix_zero * grad_one,
-                    )
-                )
-            return tuple(done)
-
-        zeros = jnp.zeros((ch_size, LANES), F32)
-        carry = ((zeros,) * 4,) * 2
-        if seq_size <= 8 or seq_ranks(seq_size) != tuple(range(seq_size)):
-            for e in range(seq_size):
-                carry = pairs(seq_ranks(seq_size).index(e), carry)
-        else:
-            carry = lax.fori_loop(0, seq_size, pairs, carry)
-        sums = [jnp.sum(carry[0][i] + carry[1][i], axis=0, keepdims=True) for i in (2, 3)]
-        extras = jnp.sum(strided(8, ch_size * seq_size, block), axis=0, keepdims=True)
-        kind = iota((8, LANES), 0)
-        sums = jnp.where(kind == 0, sums[0], sums[1])
-        shift = LANES // 2
-        while shift >= modes:
-            sums = sums + roll(sums, shift)
-            shift //= 2
-        sum_zero = sums[0:1, :modes] + extras[:, :modes]
-        sum_one = sums[1:2, :modes] + roll(extras, -modes)[:, :modes]
-        scale = jnp.sqrt(2.0 * inv) / math.sqrt(ch_size * channels * seq_size * local_len)
-        skip = jnp.sum(strided(me + 8, seq_size, block), axis=0, keepdims=True)
+        skip = jnp.sum(strided(all_ref, me + BLOCK - 1, seq_size, BLOCK), axis=0, keepdims=True)
         skip = roll(skip, -2 * modes)[:, :channels] / math.sqrt(seq_size * local_len)
-
         for i, (gate_ref, data) in enumerate(
             ((q_ref, mixed), (k_ref, grad_values), (d_ref, mixed), (x_ref, grad_values))
         ):
@@ -323,17 +338,15 @@
                 lanes = slice(j * LANES, (j + 1) * LANES)
                 part = gate_ref[:, lanes].astype(F32) * data[j * channels : (j + 1) * channels]
                 scratch[i][:, lanes] = part.astype(BF16)
-        grad_skip_ref[...] = skip
-        grad_residue_ref[...] = scale * sum_zero
-        grad_memory_ref[...] = residue_ref[...] * scale * (sum_one - 0.5 * sum_zero)
+        scratch[4][...] = skip
         for move in moves:
             move.start()
 
-    @pl.when(is_early(seq_size))
+    @pl.when(is_early())
     def _():
         complete(*early)
 
-    @pl.when(jnp.logical_not(is_early(seq_size)))
+    @pl.when(jnp.logical_not(is_early()))
     def _():
         prepare(seq_size, *arguments, *late)
         complete(*late)
@@ -353,26 +366,51 @@
     arguments = [pltpu.with_memory_space_constraint(data, pltpu.HBM) for data in arguments]
     copies = [(data.shape, data.dtype) for data in arguments]
     rows = local_len // LANES * channels
+    chips = ch_size // CORES
+    peers = chips * seq_size
     tables = [((2 * seq_size + 8, LANES), F32), ((2 * rows, LANES), F32), ((2 * LANES, 2 * LANES), BF16)]
-    mine, *rest = pl.pallas_call(
+    mine, rates, *rest = pl.pallas_call(
         functools.partial(make_states, seq_size),
         in_specs=[in_hbm] * 7,
-        out_shape=[jax.ShapeDtypeStruct(*shape) for shape in [((devices * 9, LANES), F32), *copies, *tables]],
+        out_shape=[
+            jax.ShapeDtypeStruct(*shape)
+            for shape in [((peers * BLOCK, LANES), F32), ((8, LANES), F32), *copies, *tables]
+        ],
         scratch_shapes=[pltpu.SemaphoreType.DMA((7,))],
         compiler_params=params,
     )(*arguments)
-    order = [s * ch_size + c for c in ch_ranks(ch_size) for s in seq_ranks(seq_size)]
-    everyone = lax.all_to_all(mine.reshape(devices, 9, 1, LANES), AXES, 0, 0, axis_index_groups=[order])
+    copied, tables_here = rest[:7], rest[7:]
+    groups = [
+        [s * ch_size + chip * CORES + core for chip in chip_ranks(chips) for s in seq_ranks(seq_size)]
+        for core in range(CORES)
+    ]
+    everyone = lax.all_to_all(mine.reshape(peers, BLOCK, 1, LANES), AXES, 0, 0, axis_index_groups=groups)
+    everyone = everyone.reshape(peers * BLOCK, LANES)
+    sums = pl.pallas_call(
+        functools.partial(pair_sums, seq_size, chips),
+        out_shape=jax.ShapeDtypeStruct((1, LANES), F32),
+        compiler_params=params,
+    )(rates, everyone)
+    other = lax.ppermute(sums, "ch", [(i, i ^ 1) for i in range(ch_size)])
     big = ((channels, local_len), BF16)
-    shapes = [big] * 4 + [((1, channels), F32), ((1, modes), F32), ((1, modes), F32)]
+    shapes = [big] * 4 + [((1, channels), F32)]
     results = pl.pallas_call(
         functools.partial(finish, seq_size, ch_size),
         out_shape=[jax.ShapeDtypeStruct(*shape) for shape in shapes],
-        out_specs=[in_hbm] * 7,
-        scratch_shapes=[*[pltpu.VMEM(*shape) for shape in shapes + tables], pltpu.SemaphoreType.DMA((7,))],
+        out_specs=[in_hbm] * 5,
+        scratch_shapes=[*[pltpu.VMEM(*shape) for shape in shapes + tables], pltpu.SemaphoreType.DMA((5,))],
         compiler_params=params,
-    )(*rest[:7], everyone.reshape(devices * 9, LANES), *rest[7:])
-    return (*results[:4], *[result[0] for result in results[4:]])
+        cost_estimate=pl.CostEstimate(flops=20_000_000, bytes_accessed=1_000_000, transcendentals=10_000),
+    )(*copied, everyone, *tables_here)
+    small = [((1, modes), F32)] * 2
+    filters = pl.pallas_call(
+        functools.partial(filter_grads, ch_size * channels * seq_size * local_len),
+        out_shape=[jax.ShapeDtypeStruct(*shape) for shape in small],
+        out_specs=[in_hbm] * 2,
+        scratch_shapes=[*[pltpu.VMEM(*shape) for shape in small], pltpu.SemaphoreType.DMA((2,))],
+        compiler_params=params,
+    )(copied[0], copied[1], sums, other)
+    return (*results[:4], results[4][0], filters[0][0], filters[1][0])
 
 
 def solution(mesh):

time: 17.3 us -> 16.3 us (0.942)
  blocking collectives: 13.8 us -> 11.7 us
  Pallas kernels: 2.64 us -> 3.45 us
  waiting for transfers between devices: 0 us -> 0.26 us
    all_to_all x1, blocking collectives: 13.8 us -> 11.7 us  [per_device(): lax.all_to_all(mine.reshape(peers, BLOCK, 1, LANES), AXES, 0, 0, axis_ind...]
    pallas_call x0 -> x2, Pallas kernels: none -> 0.85 us  [the longest x1 0.6 us: per_device(): pl.pallas_call(functools.partial(filter_grads, ch_size * channels * seq_s...]
    ppermute x0 -> x1, waiting for transfers between devices: none -> 0.26 us  [per_device(): other = lax.ppermute(sums, 'ch', [(i, i ^ 1) for i in range(ch_size)])]
  transfers between devices with their start and end apart: 0 -> 1, of which waited for: 0 -> 1; matrix products, arithmetic and copies ran while one was open for 0% -> 0% of each run, Pallas kernels for 0% -> 5%
where the time goes in v4:
time: 16.3 us; the launch traced here: 16.1 us
  blocking collectives  11.7 us (72%)
  Pallas kernels  3.45 us (21%)
  between operations  0.65 us (4%)
  waiting for transfers between devices  0.26 us (2%)
    all_to_all x1, blocking collectives, per_device(): lax.all_to_all(mine.reshape(peers, BLOCK, 1, LANES), AXES, 0, 0, axis_ind...  11.7 us
    pallas_call x1, Pallas kernels, per_device(): pl.pallas_call(functools.partial(make_states, seq_size), in_specs=[in_hbm...  1.76 us
    pallas_call x1, Pallas kernels, per_device(): pl.pallas_call(functools.partial(finish, seq_size, ch_size), out_shape=[j...  0.85 us
    pallas_call x1, Pallas kernels, per_device(): pl.pallas_call(functools.partial(filter_grads, ch_size * channels * seq_s...  0.6 us
  transfers between devices with their start and end apart: 1, of which 1 were waited for; matrix products, arithmetic and copies ran while one was open for 0% of the time, Pallas kernels for 5%

profile of v4, /device:TPU:0, one launch (start us, length us, event | category | flops | bytes accessed | tf_op | source)
XLA Modules:
  0.0 16.1 jit_solution(11445606099816092947)
XLA Ops:
  0.6 1.8 %shard_map.126 = (f32[144,128]{1,0:T(8,128)S(1)}, f32[8,128]{1,0:T(8,128)S(1)}, f32[1,16]{1,0:T(1,128)S(1)}, f32[1,16]{1,0:T(1,128)S(1)}, f32[1,16]{1,0:T(1,128)...) custom-call(f32[1,16]{1,0:T(1,128)} %bitcast.11, ...), custom_call_target="tpu_custom_call" | custom-call | tf_op jit(solution)/shard_map/pallas_call | solution.py:372
  2.4 11.7 %all_to_all.5 = f32[16,9,1,128]{3,2,1,0:T(1,128)S(1)} all-to-all(f32[16,9,1,128]{3,2,1,0:T(1,128)S(1)} %bitcast.10), channel_id=1, replica_groups={{30,2,6,18,26,14,10,22,28,0,4,16,24,12,8,20},{31,3,7,19,27,15,11,23,29,..., dimensions={0} | all-to-all | bytes 147456 | tf_op jit(solution)/shard_map/all_to_all | solution.py:387
  14.1 0.2 %shard_map.128.mine_ref = f32[1,128]{1,0:T(1,128)S(1)} custom-call(f32[8,128]{1,0:T(8,128)S(1)} %get-tuple-element.42.rates_ref, f32[144,128]{1,0:T(8,128)S(1)} %bitcast.8), custom_call_target="tpu_custom_call" | custom-call | tf_op jit(solution)/shard_map/pallas_call | solution.py:389
  14.4 0.0 collective-permute-start
  14.4 0.8 %shard_map.127 = (bf16[16,512]{1,0:T(8,128)(2,1)}, bf16[16,512]{1,0:T(8,128)(2,1)}, bf16[16,512]{1,0:T(8,128)(2,1)}, bf16[16,512]{1,0:T(8,128)(2,1)}, f32[1,16]{1,0:T(1,128)}) custom-call(f32[1,16]{1,0:T(1,128)S(1)} %get-tuple-element.26.refs_0_.memory_ref, f32[1,16]{1,0:T(1,128)S(1)} %get-tuple-element.27.refs_1_.residue_ref, ...), custom_call_target="tpu_custom_call" | custom-call | flops 20000000 | bytes 1000000 | tf_op jit(solution)/shard_map/pallas_call | solution.py:397
  15.2 0.3 %collective-permute-done.other_ref = f32[1,128]{1,0:T(1,128)S(1)} collective-permute-done((f32[1,128]{1,0:T(1,128)S(1)}, f32[1,128]{1,0:T(1,128)S(1)}, u32[]{:S(2)}, u32[]{:S(2)}) %collective-permute-start) | collective-permute-done | bytes 544 | tf_op jit(solution)/shard_map/ppermute | solution.py:394
  15.5 0.6 %shard_map.129 = (f32[1,16]{1,0:T(1,128)}, f32[1,16]{1,0:T(1,128)}) custom-call(f32[1,16]{1,0:T(1,128)S(1)} %get-tuple-element.26.refs_0_.memory_ref, f32[1,16]{1,0:T(1,128)S(1)} %get-tuple-element.27.refs_1_.residue_ref, f32[1,128]{1,0:T(1,128)S(1)} %shard_map.128.mine_ref, f32[1,128]{1,0:T(1,128)S(1)} %collective-permute-done.other_ref), custom_call_target="tpu_custom_call" | custom-call | tf_op jit(solution)/shard_map/pallas_call | solution.py:406
Async XLA Ops:
  14.4 1.1 %collective-permute-start = (f32[1,128]{1,0:T(1,128)S(1)}, f32[1,128]{1,0:T(1,128)S(1)}, u32[]{:S(2)}, u32[]{:S(2)}) collective-permute-start(f32[1,128]{1,0:T(1,128)S(1)} %shard_map.128.mine_ref), channel_id=1, source_target_pairs={{0,1},{1,0},{2,3},{3,2},{4,5},{5,4},{6,7},{7,6},{8,9},{9,8},{10,11... | collective-permute-start | bytes 1544 | tf_op jit(solution)/shard_map/ppermute | solution.py:394

commit v5 on v4

--- a/solution.py
+++ b/solution.py
@@ -268,13 +268,9 @@
         carry = lax.fori_loop(0, seq_size, pairs, carry)
     sums = [jnp.sum(carry[0][i] + carry[1][i], axis=0, keepdims=True) for i in (2, 3)]
     extras = jnp.sum(strided(all_ref, BLOCK - 1, chips * seq_size, BLOCK), axis=0, keepdims=True)
-    sums = jnp.where(iota((8, LANES), 0) == 0, sums[0], sums[1])
-    shift = LANES // 2
-    while shift >= modes:
-        sums = sums + roll(sums, shift)
-        shift //= 2
-    lane = iota((1, LANES), 1)
-    sums_ref[...] = extras + jnp.where(lane < modes, sums[0:1], jnp.where(lane < 2 * modes, sums[1:2], 0.0))
+    kind = iota((8, LANES), 0)
+    sums = jnp.where(kind == 0, sums[0], sums[1]) + jnp.where(iota((8, LANES), 1) // modes == kind, extras, 0.0)
+    sums_ref[...] = sum([roll(sums, shift) for shift in range(modes, LANES, modes)], sums)
 
 
 def filter_grads(total, memory_ref, residue_ref, mine_ref, other_ref, *refs):
@@ -282,7 +278,7 @@
     modes = memory_ref.shape[1]
     scale = jnp.sqrt(2.0 / memory_ref[...]) / math.sqrt(total)
     sums = mine_ref[...] + other_ref[...]
-    sum_zero, sum_one = sums[:, :modes], roll(sums, -modes)[:, :modes]
+    sum_zero, sum_one = sums[0:1, :modes], sums[1:2, :modes]
     scratch[0][...] = scale * sum_zero
     scratch[1][...] = residue_ref[...] * scale * (sum_one - 0.5 * sum_zero)
     moves = [pltpu.make_async_copy(*ends, sent.at[i]) for i, ends in enumerate(zip(scratch, results))]
@@ -388,7 +384,7 @@
     everyone = everyone.reshape(peers * BLOCK, LANES)
     sums = pl.pallas_call(
         functools.partial(pair_sums, seq_size, chips),
-        out_shape=jax.ShapeDtypeStruct((1, LANES), F32),
+        out_shape=jax.ShapeDtypeStruct((8, LANES), F32),
         compiler_params=params,
     )(rates, everyone)
     other = lax.ppermute(sums, "ch", [(i, i ^ 1) for i in range(ch_size)])

time: 16.3 us -> 16.2 us (level)
  Pallas kernels: 3.45 us -> 3.28 us
where the time goes in v5:
time: 16.2 us; the launch traced here: 15.9 us
  blocking collectives  11.7 us (72%)
  Pallas kernels  3.28 us (20%)
  between operations  0.66 us (4%)
  waiting for transfers between devices  0.28 us (2%)
    all_to_all x1, blocking collectives, per_device(): lax.all_to_all(mine.reshape(peers, BLOCK, 1, LANES), AXES, 0, 0, axis_ind...  11.7 us
    pallas_call x1, Pallas kernels, per_device(): pl.pallas_call(functools.partial(make_states, seq_size), in_specs=[in_hbm...  1.76 us
    pallas_call x1, Pallas kernels, per_device(): pl.pallas_call(functools.partial(finish, seq_size, ch_size), out_shape=[j...  0.86 us
    pallas_call x1, Pallas kernels, per_device(): pl.pallas_call(functools.partial(filter_grads, ch_size * channels * seq_s...  0.55 us
  transfers between devices with their start and end apart: 1, of which 1 were waited for; matrix products, arithmetic and copies ran while one was open for 0% of the time, Pallas kernels for 5%

profile of v5, /device:TPU:0, one launch (start us, length us, event | category | flops | bytes accessed | tf_op | source)
XLA Modules:
  0.0 15.9 jit_solution(562656601379302819)
XLA Ops:
  0.6 1.8 %shard_map.126 = (f32[144,128]{1,0:T(8,128)S(1)}, f32[8,128]{1,0:T(8,128)S(1)}, f32[1,16]{1,0:T(1,128)S(1)}, f32[1,16]{1,0:T(1,128)S(1)}, f32[1,16]{1,0:T(1,128)...) custom-call(f32[1,16]{1,0:T(1,128)} %bitcast.11, ...), custom_call_target="tpu_custom_call" | custom-call | tf_op jit(solution)/shard_map/pallas_call | solution.py:368
  2.4 11.7 %all_to_all.5 = f32[16,9,1,128]{3,2,1,0:T(1,128)S(1)} all-to-all(f32[16,9,1,128]{3,2,1,0:T(1,128)S(1)} %bitcast.10), channel_id=1, replica_groups={{30,2,6,18,26,14,10,22,28,0,4,16,24,12,8,20},{31,3,7,19,27,15,11,23,29,..., dimensions={0} | all-to-all | bytes 147456 | tf_op jit(solution)/shard_map/all_to_all | solution.py:383
  14.1 0.1 shard_map.128.mine_ref
  14.2 0.0 collective-permute-start
  14.2 0.9 %shard_map.127 = (bf16[16,512]{1,0:T(8,128)(2,1)}, bf16[16,512]{1,0:T(8,128)(2,1)}, bf16[16,512]{1,0:T(8,128)(2,1)}, bf16[16,512]{1,0:T(8,128)(2,1)}, f32[1,16]{1,0:T(1,128)}) custom-call(f32[1,16]{1,0:T(1,128)S(1)} %get-tuple-element.26.refs_0_.memory_ref, f32[1,16]{1,0:T(1,128)S(1)} %get-tuple-element.27.refs_1_.residue_ref, ...), custom_call_target="tpu_custom_call" | custom-call | flops 20000000 | bytes 1000000 | tf_op jit(solution)/shard_map/pallas_call | solution.py:393
  15.1 0.3 %collective-permute-done.other_ref = f32[8,128]{1,0:T(8,128)S(1)} collective-permute-done((f32[8,128]{1,0:T(8,128)S(1)}, f32[8,128]{1,0:T(8,128)S(1)}, u32[]{:S(2)}, u32[]{:S(2)}) %collective-permute-start) | collective-permute-done | bytes 4128 | tf_op jit(solution)/shard_map/ppermute | solution.py:390
  15.4 0.5 %shard_map.129 = (f32[1,16]{1,0:T(1,128)}, f32[1,16]{1,0:T(1,128)}) custom-call(f32[1,16]{1,0:T(1,128)S(1)} %get-tuple-element.26.refs_0_.memory_ref, f32[1,16]{1,0:T(1,128)S(1)} %get-tuple-element.27.refs_1_.residue_ref, f32[8,128]{1,0:T(8,128)S(1)} %shard_map.128.mine_ref, f32[8,128]{1,0:T(8,128)S(1)} %collective-permute-done.other_ref), custom_call_target="tpu_custom_call" | custom-call | tf_op jit(solution)/shard_map/pallas_call | solution.py:402
Async XLA Ops:
  14.2 1.2 %collective-permute-start = (f32[8,128]{1,0:T(8,128)S(1)}, f32[8,128]{1,0:T(8,128)S(1)}, u32[]{:S(2)}, u32[]{:S(2)}) collective-permute-start(f32[8,128]{1,0:T(8,128)S(1)} %shard_map.128.mine_ref), channel_id=1, source_target_pairs={{0,1},{1,0},{2,3},{3,2},{4,5},{5,4},{6,7},{7,6},{8,9},{9,8},{10,11... | collective-permute-start | bytes 12296 | tf_op jit(solution)/shard_map/ppermute | solution.py:390

commit v6 on v5

--- a/solution.py
+++ b/solution.py
@@ -85,29 +85,26 @@
     return ranks(chips, (1, 0))
 
 
-def is_early():
-    return (lax.axis_index("seq") == 0) & (lax.axis_index("ch") < CORES)
-
-
 def strided(ref, start, count, stride):
     return ref[pl.ds(start, count, stride=stride), :]
 
 
-def prepare(seq_size, memory_ref, residue_ref, skip_ref, x_ref, q_ref, k_ref, d_ref, table_ref, base_ref, read_ref):
-    modes = memory_ref.shape[1]
-    channels, local_len = x_ref.shape
-    chunks = local_len // LANES
+def local_parts(seq_size, rates_ref, values, grads, parameters, chunks, channels):
     rows = chunks * channels
+    modes = (rates_ref.shape[0] - 8) // 2
+    local_len = chunks * LANES
     me_seq = lax.axis_index("seq")
-    inv = 1.0 / memory_ref[...]
-    inv_col = column(inv)
-    inv_row = tiled_row(inv_col)
-    decay_in, _, decay_out, _ = decays(inv_col)
-    amplitude = column(residue_ref[...] * jnp.sqrt(2.0 * inv))
-    values = by_chunk(x_ref) * by_chunk(k_ref)
-    grads = by_chunk(d_ref) * by_chunk(q_ref)
+    inv_row = rates_ref[2:3]
+    memory_ref, residue_ref, skip_ref = parameters
+    amplitude = column(residue_ref[...] * jnp.sqrt(2.0 / memory_ref[...]))
+    read_in, read_out = amplitude * rates_ref[8 : 8 + modes], amplitude * rates_ref[8 + modes :]
     value_split = left_split(values)
     grad_split = left_split(grads)
+
+    taps = jnp.sum(read_out, axis=0, keepdims=True)
+    square = (LANES, LANES)
+    toeplitz = pltpu.roll(jnp.broadcast_to(taps, square), 0, 1, stride=1, stride_axis=0)
+    toeplitz = jnp.where(iota(square, 1) >= iota(square, 0), toeplitz, 0.0)
 
     device = iota((seq_size, LANES), 0)
     if seq_ranks(seq_size) != tuple(range(seq_size)):
@@ -116,43 +113,17 @@
             device = jnp.where(place == p, index, device)
     ahead = (me_seq - 1 - device).astype(F32) * local_len
     behind = (device - me_seq - 1).astype(F32) * local_len
-    table_ref[:seq_size] = jnp.where(ahead >= 0, jnp.exp(-jnp.maximum(ahead, 0.0) * inv_row), 0.0)
-    table_ref[seq_size : 2 * seq_size] = jnp.where(behind >= 0, jnp.exp(-jnp.maximum(behind, 0.0) * inv_row), 0.0)
-    power = iota((chunks, LANES), 0).astype(F32) * LANES
-    table_ref[2 * seq_size : 2 * seq_size + chunks] = jnp.exp(-power * inv_row)
-
-    read_in, read_out = tile_modes(amplitude * decay_in), tile_modes(amplitude * decay_out)
-    read_ref[:LANES] = jnp.concatenate(halves(read_out), axis=1)
-    read_ref[LANES:] = jnp.concatenate(halves(read_in), axis=1)
-
-    value_states = contract(value_split, right_split(tile_modes(decay_in)), 1, 1)
-    grad_states = contract(grad_split, right_split(tile_modes(decay_out)), 1, 1)
-    step = jnp.exp(-LANES * inv_row)
-    starts, ends = [jnp.zeros((channels, LANES), F32)], [jnp.zeros((channels, LANES), F32)]
-    for j in range(chunks - 1):
-        starts.append(step * starts[-1] + value_states[j * channels : (j + 1) * channels])
-        i = chunks - 1 - j
-        ends.append(step * ends[-1] + grad_states[i * channels : (i + 1) * channels])
-    first = iota((rows, LANES), 1) < modes
-
-    def state_split(parts):
-        return left_split(jnp.where(first, jnp.concatenate(parts, axis=0), 0.0))
-
-    taps = jnp.sum(amplitude * decay_out, axis=0, keepdims=True)
-    square = (LANES, LANES)
-    toeplitz = pltpu.roll(jnp.broadcast_to(taps, square), 0, 1, stride=1, stride_axis=0)
-    toeplitz = jnp.where(iota(square, 1) >= iota(square, 0), toeplitz, 0.0)
+    weights = [jnp.where(far >= 0, jnp.exp(-jnp.maximum(far, 0.0) * inv_row), 0.0) for far in (ahead, behind)]
+    powers = [jnp.exp(-float(j * LANES) * inv_row) for j in range(chunks)]
+
     conv = contract(value_split, right_split(toeplitz, axis=0), 1, 0)
-    conv = conv + contract(state_split(starts), right_split(read_out, axis=0), 1, 0)
     corr = contract(grad_split, right_split(toeplitz), 1, 1)
-    corr = corr + contract(state_split(ends[::-1]), right_split(read_in, axis=0), 1, 0)
     gain = jnp.concatenate([column(skip_ref[...])] * chunks, axis=0)
-    base_ref[:rows] = conv + gain * values
-    base_ref[rows:] = corr + gain * grads
-
-
-def make_states(seq_size, *refs):
-    sources, (out_ref, rates_ref, *copies), tables, arrived = refs[:7], refs[7:16], refs[16:19], refs[19]
+    return weights, powers, conv + gain * values, corr + gain * grads, tile_modes(read_out), tile_modes(read_in)
+
+
+def make_states(*refs):
+    sources, (out_ref, rates_ref, starts_ref, ends_ref, *copies), arrived = refs[:7], refs[7:18], refs[18]
     moves = [pltpu.make_async_copy(*ends, arrived.at[i]) for i, ends in enumerate(zip(sources, copies))]
     for i in (0, 3, 5, 6, 4, 1, 2):
         moves[i].start()
@@ -172,6 +143,9 @@
     leap = jnp.exp(-local_len * inv_row)
     rates_ref[0:1] = leap
     rates_ref[1:2] = leap * (local_len * inv_row)
+    rates_ref[2:3] = inv_row
+    rates_ref[8 : 8 + modes] = decay_in
+    rates_ref[8 + modes :] = decay_out
     moves[3].wait()
     moves[5].wait()
     values = by_chunk(x_ref) * by_chunk(k_ref)
@@ -196,18 +170,20 @@
     row_id = iota((channels, LANES), 0)
     prefix_zero = jnp.zeros((channels, LANES), F32)
     prefix_one = cross_zero = cross_one = suffix_zero = suffix_one = prefix_zero
-    power = jnp.ones_like(step)
     for j in range(chunks):
         rows = slice(j * channels, (j + 1) * channels)
         grad_zero, grad_one = grad_states[rows, :LANES], grad_states[rows, LANES:]
         if j > 0:
             cross_zero = cross_zero + prefix_zero * grad_zero
             cross_one = cross_one + prefix_one * grad_zero + prefix_zero * grad_one
+        starts_ref[rows] = prefix_zero
         prefix_one = step * (prefix_one + growth * prefix_zero) + value_states[rows, LANES:]
         prefix_zero = step * prefix_zero + value_states[rows, :LANES]
-        suffix_zero = suffix_zero + power * grad_zero
-        suffix_one = suffix_one + power * (grad_one + j * growth * grad_zero)
-        power = power * step
+    for j in range(chunks - 1, -1, -1):
+        rows = slice(j * channels, (j + 1) * channels)
+        ends_ref[rows] = suffix_zero
+        suffix_one = step * (suffix_one + growth * suffix_zero) + grad_states[rows, LANES:]
+        suffix_zero = step * suffix_zero + grad_states[rows, :LANES]
     half = channels // 2
     own = lane // modes == row_id % half
     payload = []
@@ -234,10 +210,6 @@
     for move in moves[1:3]:
         move.wait()
 
-    @pl.when(is_early())
-    def _():
-        prepare(seq_size, *copies, *tables)
-
 
 def pair_sums(seq_size, chips, rates_ref, all_ref, sums_ref):
     modes = LANES // 8
@@ -288,65 +260,49 @@
         move.wait()
 
 
-def finish(seq_size, ch_size, *refs):
-    arguments, all_ref, early, refs = refs[:7], refs[7], refs[8:11], refs[11:]
-    results, scratch, late, sent = refs[:5], refs[5:10], refs[10:13], refs[13]
-    _, _, _, x_ref, q_ref, k_ref, d_ref = arguments
+def finish(seq_size, ch_size, rates_ref, starts_ref, ends_ref, *refs):
+    parameters, (x_ref, q_ref, k_ref, d_ref, all_ref), refs = refs[:3], refs[3:8], refs[8:]
+    results, scratch, sent = refs[:5], refs[5:10], refs[10]
     moves = [pltpu.make_async_copy(*ends, sent.at[i]) for i, ends in enumerate(zip(scratch, results))]
     channels, local_len = x_ref.shape
     modes = LANES // 8
     chunks = local_len // LANES
     half = channels // 2
     rows = chunks * channels
-
-    def complete(table_ref, base_ref, read_ref):
-        me = 0
-        for p, index in enumerate(chip_ranks(ch_size // CORES)):
-            me = me + jnp.where(lax.axis_index("ch") // CORES == index, p * seq_size * BLOCK, 0)
-        own = iota((half, LANES), 1) // modes == iota((half, LANES), 0)
-
-        def border(kind, weights):
-            parts = []
-            for part in range(2):
-                state = strided(all_ref, me + 2 * kind + part, seq_size, BLOCK)
-                state = jnp.sum(weights * state, axis=0, keepdims=True)
-                parts.append(jnp.where(own, state, 0.0))
-            return jnp.concatenate(parts, axis=0)
-
-        before = border(0, table_ref[:seq_size])
-        after = border(2, table_ref[seq_size : 2 * seq_size])
-        powers = [table_ref[2 * seq_size + j : 2 * seq_size + j + 1] for j in range(chunks)]
-
-        def readout(state, factors, matrix):
-            high, low = halves(jnp.concatenate([factor * state for factor in factors], axis=0))
-            product = contract(jnp.concatenate([high, low], axis=0), matrix, 1, 0)
-            return product[:rows, :LANES] + product[:rows, LANES:] + product[rows:, :LANES]
-
-        mixed = base_ref[:rows] + readout(before, powers, read_ref[:LANES])
-        grad_values = base_ref[rows:] + readout(after, powers[::-1], read_ref[LANES:])
-
-        skip = jnp.sum(strided(all_ref, me + BLOCK - 1, seq_size, BLOCK), axis=0, keepdims=True)
-        skip = roll(skip, -2 * modes)[:, :channels] / math.sqrt(seq_size * local_len)
-        for i, (gate_ref, data) in enumerate(
-            ((q_ref, mixed), (k_ref, grad_values), (d_ref, mixed), (x_ref, grad_values))
-        ):
-            for j in range(chunks):
-                lanes = slice(j * LANES, (j + 1) * LANES)
-                part = gate_ref[:, lanes].astype(F32) * data[j * channels : (j + 1) * channels]
-                scratch[i][:, lanes] = part.astype(BF16)
-        scratch[4][...] = skip
-        for move in moves:
-            move.start()
-
-    @pl.when(is_early())
-    def _():
-        complete(*early)
-
-    @pl.when(jnp.logical_not(is_early()))
-    def _():
-        prepare(seq_size, *arguments, *late)
-        complete(*late)
-
+    signal, gate_in = by_chunk(x_ref), by_chunk(k_ref)
+    gate_out, cotangent = by_chunk(q_ref), by_chunk(d_ref)
+    weights, powers, base_mixed, base_grad, read_out, read_in = local_parts(
+        seq_size, rates_ref, signal * gate_in, cotangent * gate_out, parameters, chunks, channels
+    )
+    me = 0
+    for p, index in enumerate(chip_ranks(ch_size // CORES)):
+        me = me + jnp.where(lax.axis_index("ch") // CORES == index, p * seq_size * BLOCK, 0)
+    own = iota((half, LANES), 1) // modes == iota((half, LANES), 0)
+
+    def border(kind, weight):
+        parts = []
+        for part in range(2):
+            state = strided(all_ref, me + 2 * kind + part, seq_size, BLOCK)
+            state = jnp.sum(weight * state, axis=0, keepdims=True)
+            parts.append(jnp.where(own, state, 0.0))
+        return jnp.concatenate(parts, axis=0)
+
+    mine = iota((rows, LANES), 1) // modes == iota((rows, LANES), 0) % half
+
+    def readout(state, factors, states, matrix):
+        state = jnp.concatenate([factor * state for factor in factors], axis=0) + jnp.where(mine, states, 0.0)
+        return contract(left_split(state), right_split(matrix, axis=0), 1, 0)
+
+    mixed = base_mixed + readout(border(0, weights[0]), powers, starts_ref[...], read_out)
+    grad_values = base_grad + readout(border(2, weights[1]), powers[::-1], ends_ref[...], read_in)
+    skip = jnp.sum(strided(all_ref, me + BLOCK - 1, seq_size, BLOCK), axis=0, keepdims=True)
+    skip = roll(skip, -2 * modes)[:, :channels] / math.sqrt(seq_size * local_len)
+    for i, data in enumerate((gate_out * mixed, grad_values * gate_in, cotangent * mixed, grad_values * signal)):
+        for j in range(chunks):
+            scratch[i][:, j * LANES : (j + 1) * LANES] = data[j * channels : (j + 1) * channels].astype(BF16)
+    scratch[4][...] = skip
+    for move in moves:
+        move.start()
     for move in moves:
         move.wait()
 
@@ -364,18 +320,14 @@
     rows = local_len // LANES * channels
     chips = ch_size // CORES
     peers = chips * seq_size
-    tables = [((2 * seq_size + 8, LANES), F32), ((2 * rows, LANES), F32), ((2 * LANES, 2 * LANES), BF16)]
-    mine, rates, *rest = pl.pallas_call(
-        functools.partial(make_states, seq_size),
+    made = [((peers * BLOCK, LANES), F32), ((8 + 2 * modes, LANES), F32), ((rows, LANES), F32), ((rows, LANES), F32)]
+    mine, rates, starts, ends, *copied = pl.pallas_call(
+        make_states,
         in_specs=[in_hbm] * 7,
-        out_shape=[
-            jax.ShapeDtypeStruct(*shape)
-            for shape in [((peers * BLOCK, LANES), F32), ((8, LANES), F32), *copies, *tables]
-        ],
+        out_shape=[jax.ShapeDtypeStruct(*shape) for shape in made + copies],
         scratch_shapes=[pltpu.SemaphoreType.DMA((7,))],
         compiler_params=params,
     )(*arguments)
-    copied, tables_here = rest[:7], rest[7:]
     groups = [
         [s * ch_size + chip * CORES + core for chip in chip_ranks(chips) for s in seq_ranks(seq_size)]
         for core in range(CORES)
@@ -394,10 +346,10 @@
         functools.partial(finish, seq_size, ch_size),
         out_shape=[jax.ShapeDtypeStruct(*shape) for shape in shapes],
         out_specs=[in_hbm] * 5,
-        scratch_shapes=[*[pltpu.VMEM(*shape) for shape in shapes + tables], pltpu.SemaphoreType.DMA((5,))],
+        scratch_shapes=[*[pltpu.VMEM(*shape) for shape in shapes], pltpu.SemaphoreType.DMA((5,))],
         compiler_params=params,
         cost_estimate=pl.CostEstimate(flops=20_000_000, bytes_accessed=1_000_000, transcendentals=10_000),
-    )(*copied, everyone, *tables_here)
+    )(rates, starts, ends, *copied, everyone)
     small = [((1, modes), F32)] * 2
     filters = pl.pallas_call(
         functools.partial(filter_grads, ch_size * channels * seq_size * local_len),

time: 16.2 us -> 16.2 us (level)
  blocking collectives: 11.7 us -> 12.2 us
  Pallas kernels: 3.28 us -> 3.02 us
  waiting for transfers between devices: 0.28 us -> 0.05 us
    pallas_call x1, Pallas kernels: 1.76 us -> 1.26 us  [per_device(): pl.pallas_call(make_states, in_specs=[in_hbm] * 7, out_shape=[jax.ShapeDt...]
    all_to_all x1, blocking collectives: 11.7 us -> 12.2 us  [per_device(): lax.all_to_all(mine.reshape(peers, BLOCK, 1, LANES), AXES, 0, 0, axis_ind...]
    pallas_call x1, Pallas kernels: 0.86 us -> 1.1 us  [per_device(): pl.pallas_call(functools.partial(finish, seq_size, ch_size), out_shape=[j...]
    ppermute x1, waiting for transfers between devices: 0.28 us -> 0.05 us  [per_device(): other = lax.ppermute(sums, 'ch', [(i, i ^ 1) for i in range(ch_size)])]
  transfers between devices with their start and end apart: 1 -> 1, of which waited for: 1 -> 0; matrix products, arithmetic and copies ran while one was open for 0% -> 0% of each run, Pallas kernels for 5% -> 7%
where the time goes in v6:
time: 16.2 us; the launch traced here: 15.9 us
  blocking collectives  12.2 us (75%)
  Pallas kernels  3.02 us (19%)
  between operations  0.66 us (4%)
    all_to_all x1, blocking collectives, per_device(): lax.all_to_all(mine.reshape(peers, BLOCK, 1, LANES), AXES, 0, 0, axis_ind...  12.2 us
    pallas_call x1, Pallas kernels, per_device(): pl.pallas_call(make_states, in_specs=[in_hbm] * 7, out_shape=[jax.ShapeDt...  1.26 us
    pallas_call x1, Pallas kernels, per_device(): pl.pallas_call(functools.partial(finish, seq_size, ch_size), out_shape=[j...  1.1 us
    pallas_call x1, Pallas kernels, per_device(): pl.pallas_call(functools.partial(filter_grads, ch_size * channels * seq_s...  0.55 us
  transfers between devices with their start and end apart: 1, of which 0 were waited for; matrix products, arithmetic and copies ran while one was open for 0% of the time, Pallas kernels for 7%

profile of v6, /device:TPU:0, one launch (start us, length us, event | category | flops | bytes accessed | tf_op | source)
XLA Modules:
  0.0 15.9 jit_solution(8639664022989634296)
XLA Ops:
  0.6 1.3 %shard_map.126 = (f32[144,128]{1,0:T(8,128)S(1)}, f32[40,128]{1,0:T(8,128)S(1)}, f32[64,128]{1,0:T(8,128)S(1)}, f32[64,128]{1,0:T(8,128)S(1)}, f32[1,16]{1,0:T(1...) custom-call(f32[1,16]{1,0:T(1,128)} %bitcast.11, ...), custom_call_target="tpu_custom_call" | custom-call | tf_op jit(solution)/shard_map/pallas_call | solution.py:324
  1.9 12.2 %all_to_all.5 = f32[16,9,1,128]{3,2,1,0:T(1,128)S(1)} all-to-all(f32[16,9,1,128]{3,2,1,0:T(1,128)S(1)} %bitcast.10), channel_id=1, replica_groups={{30,2,6,18,26,14,10,22,28,0,4,16,24,12,8,20},{31,3,7,19,27,15,11,23,29,..., dimensions={0} | all-to-all | bytes 147456 | tf_op jit(solution)/shard_map/all_to_all | solution.py:335
  14.1 0.1 shard_map.128.mine_ref
  14.2 0.0 collective-permute-start
  14.2 1.1 %shard_map.127 = (bf16[16,512]{1,0:T(8,128)(2,1)}, bf16[16,512]{1,0:T(8,128)(2,1)}, bf16[16,512]{1,0:T(8,128)(2,1)}, bf16[16,512]{1,0:T(8,128)(2,1)}, f32[1,16]{1,0:T(1,128)}) custom-call(f32[40,128]{1,0:T(8,128)S(1)} %get-tuple-element.25.rates_ref, f32[64,128]{1,0:T(8,128)S(1)} %get-tuple-element.26.starts_ref, f32[64,128]{1,0:T(8,128)S(1)} %get-tuple-element.27.ends_ref, ...), custom_call_target="tpu_custom_call" | custom-call | flops 20000000 | bytes 1000000 | tf_op jit(solution)/shard_map/pallas_call | solution.py:345
  15.3 0.0 collective-permute-done.other_ref
  15.4 0.5 %shard_map.129 = (f32[1,16]{1,0:T(1,128)}, f32[1,16]{1,0:T(1,128)}) custom-call(f32[1,16]{1,0:T(1,128)S(1)} %get-tuple-element.28.refs_0_.memory_ref, f32[1,16]{1,0:T(1,128)S(1)} %get-tuple-element.29.refs_1_.residue_ref, f32[8,128]{1,0:T(8,128)S(1)} %shard_map.128.mine_ref, f32[8,128]{1,0:T(8,128)S(1)} %collective-permute-done.other_ref), custom_call_target="tpu_custom_call" | custom-call | tf_op jit(solution)/shard_map/pallas_call | solution.py:354
Async XLA Ops:
  14.2 1.2 %collective-permute-start = (f32[8,128]{1,0:T(8,128)S(1)}, f32[8,128]{1,0:T(8,128)S(1)}, u32[]{:S(2)}, u32[]{:S(2)}) collective-permute-start(f32[8,128]{1,0:T(8,128)S(1)} %shard_map.128.mine_ref), channel_id=1, source_target_pairs={{0,1},{1,0},{2,3},{3,2},{4,5},{5,4},{6,7},{7,6},{8,9},{9,8},{10,11... | collective-permute-start | bytes 12296 | tf_op jit(solution)/shard_map/ppermute | solution.py:342

commit v7 on v6

--- a/solution.py
+++ b/solution.py
@@ -78,7 +78,7 @@
 
 
 def seq_ranks(seq_size):
-    return ranks(seq_size, (7, 0, 1, 4, 6, 3, 2, 5))
+    return ranks(seq_size, (5, 0, 4, 6, 1, 7, 2, 3))
 
 
 def chip_ranks(chips):

time: 16.2 us -> 15.9 us (0.981)
  blocking collectives: 12.2 us -> 12 us
    all_to_all x1, blocking collectives: 12.2 us -> 12 us  [per_device(): lax.all_to_all(mine.reshape(peers, BLOCK, 1, LANES), AXES, 0, 0, axis_ind...]
where the time goes in v7:
time: 15.9 us; the launch traced here: 15.7 us
  blocking collectives  12 us (75%)
  Pallas kernels  3.02 us (19%)
  between operations  0.66 us (4%)
    all_to_all x1, blocking collectives, per_device(): lax.all_to_all(mine.reshape(peers, BLOCK, 1, LANES), AXES, 0, 0, axis_ind...  12 us
    pallas_call x1, Pallas kernels, per_device(): pl.pallas_call(make_states, in_specs=[in_hbm] * 7, out_shape=[jax.ShapeDt...  1.26 us
    pallas_call x1, Pallas kernels, per_device(): pl.pallas_call(functools.partial(finish, seq_size, ch_size), out_shape=[j...  1.1 us
    pallas_call x1, Pallas kernels, per_device(): pl.pallas_call(functools.partial(filter_grads, ch_size * channels * seq_s...  0.55 us
  transfers between devices with their start and end apart: 1, of which 0 were waited for; matrix products, arithmetic and copies ran while one was open for 0% of the time, Pallas kernels for 7%

profile of v7, /device:TPU:0, one launch (start us, length us, event | category | flops | bytes accessed | tf_op | source)
XLA Modules:
  0.0 15.7 jit_solution(5317718173532008865)
XLA Ops:
  0.6 1.3 %shard_map.126 = (f32[144,128]{1,0:T(8,128)S(1)}, f32[40,128]{1,0:T(8,128)S(1)}, f32[64,128]{1,0:T(8,128)S(1)}, f32[64,128]{1,0:T(8,128)S(1)}, f32[1,16]{1,0:T(1...) custom-call(f32[1,16]{1,0:T(1,128)} %bitcast.11, ...), custom_call_target="tpu_custom_call" | custom-call | tf_op jit(solution)/shard_map/pallas_call | solution.py:324
  1.9 12.0 %all_to_all.5 = f32[16,9,1,128]{3,2,1,0:T(1,128)S(1)} all-to-all(f32[16,9,1,128]{3,2,1,0:T(1,128)S(1)} %bitcast.10), channel_id=1, replica_groups={{22,2,18,26,6,30,10,14,20,0,16,24,4,28,8,12},{23,3,19,27,7,31,11,15,21,..., dimensions={0} | all-to-all | bytes 147456 | tf_op jit(solution)/shard_map/all_to_all | solution.py:335
  13.9 0.1 shard_map.128.mine_ref
  14.0 0.0 collective-permute-start
  14.0 1.1 %shard_map.127 = (bf16[16,512]{1,0:T(8,128)(2,1)}, bf16[16,512]{1,0:T(8,128)(2,1)}, bf16[16,512]{1,0:T(8,128)(2,1)}, bf16[16,512]{1,0:T(8,128)(2,1)}, f32[1,16]{1,0:T(1,128)}) custom-call(f32[40,128]{1,0:T(8,128)S(1)} %get-tuple-element.25.rates_ref, f32[64,128]{1,0:T(8,128)S(1)} %get-tuple-element.26.starts_ref, f32[64,128]{1,0:T(8,128)S(1)} %get-tuple-element.27.ends_ref, ...), custom_call_target="tpu_custom_call" | custom-call | flops 20000000 | bytes 1000000 | tf_op jit(solution)/shard_map/pallas_call | solution.py:345
  15.1 0.0 collective-permute-done.other_ref
  15.2 0.5 %shard_map.129 = (f32[1,16]{1,0:T(1,128)}, f32[1,16]{1,0:T(1,128)}) custom-call(f32[1,16]{1,0:T(1,128)S(1)} %get-tuple-element.28.refs_0_.memory_ref, f32[1,16]{1,0:T(1,128)S(1)} %get-tuple-element.29.refs_1_.residue_ref, f32[8,128]{1,0:T(8,128)S(1)} %shard_map.128.mine_ref, f32[8,128]{1,0:T(8,128)S(1)} %collective-permute-done.other_ref), custom_call_target="tpu_custom_call" | custom-call | tf_op jit(solution)/shard_map/pallas_call | solution.py:354
Async XLA Ops:
  14.0 1.2 %collective-permute-start = (f32[8,128]{1,0:T(8,128)S(1)}, f32[8,128]{1,0:T(8,128)S(1)}, u32[]{:S(2)}, u32[]{:S(2)}) collective-permute-start(f32[8,128]{1,0:T(8,128)S(1)} %shard_map.128.mine_ref), channel_id=1, source_target_pairs={{0,1},{1,0},{2,3},{3,2},{4,5},{5,4},{6,7},{7,6},{8,9},{9,8},{10,11... | collective-permute-start | bytes 12296 | tf_op jit(solution)/shard_map/ppermute | solution.py:342

commit v8 on v7

--- a/solution.py
+++ b/solution.py
@@ -329,7 +329,7 @@
         compiler_params=params,
     )(*arguments)
     groups = [
-        [s * ch_size + chip * CORES + core for chip in chip_ranks(chips) for s in seq_ranks(seq_size)]
+        [s * ch_size + chip * CORES + (core + chip) % CORES for chip in chip_ranks(chips) for s in seq_ranks(seq_size)]
         for core in range(CORES)
     ]
     everyone = lax.all_to_all(mine.reshape(peers, BLOCK, 1, LANES), AXES, 0, 0, axis_index_groups=groups)

time: 15.9 us -> 15.8 us (level)
  no operation moved by 1% of the time
where the time goes in v8:
time: 15.8 us; the launch traced here: 15.6 us
  blocking collectives  11.9 us (75%)
  Pallas kernels  3.01 us (19%)
  between operations  0.65 us (4%)
    all_to_all x1, blocking collectives, per_device(): lax.all_to_all(mine.reshape(peers, BLOCK, 1, LANES), AXES, 0, 0, axis_ind...  11.9 us
    pallas_call x1, Pallas kernels, per_device(): pl.pallas_call(make_states, in_specs=[in_hbm] * 7, out_shape=[jax.ShapeDt...  1.26 us
    pallas_call x1, Pallas kernels, per_device(): pl.pallas_call(functools.partial(finish, seq_size, ch_size), out_shape=[j...  1.09 us
    pallas_call x1, Pallas kernels, per_device(): pl.pallas_call(functools.partial(filter_grads, ch_size * channels * seq_s...  0.55 us
  transfers between devices with their start and end apart: 1, of which 0 were waited for; matrix products, arithmetic and copies ran while one was open for 0% of the time, Pallas kernels for 7%

profile of v8, /device:TPU:0, one launch (start us, length us, event | category | flops | bytes accessed | tf_op | source)
XLA Modules:
  0.0 15.6 jit_solution(15015139749337097530)
XLA Ops:
  0.6 1.3 %shard_map.126 = (f32[144,128]{1,0:T(8,128)S(1)}, f32[40,128]{1,0:T(8,128)S(1)}, f32[64,128]{1,0:T(8,128)S(1)}, f32[64,128]{1,0:T(8,128)S(1)}, f32[1,16]{1,0:T(1...) custom-call(f32[1,16]{1,0:T(1,128)} %bitcast.11, ...), custom_call_target="tpu_custom_call" | custom-call | tf_op jit(solution)/shard_map/pallas_call | solution.py:324
  1.9 11.9 %all_to_all.5 = f32[16,9,1,128]{3,2,1,0:T(1,128)S(1)} all-to-all(f32[16,9,1,128]{3,2,1,0:T(1,128)S(1)} %bitcast.10), channel_id=1, replica_groups={{23,3,19,27,7,31,11,15,20,0,16,24,4,28,8,12},{22,2,18,26,6,30,10,14,21,..., dimensions={0} | all-to-all | bytes 147456 | tf_op jit(solution)/shard_map/all_to_all | solution.py:335
  13.8 0.1 shard_map.128.mine_ref
  13.9 0.0 collective-permute-start
  13.9 1.1 %shard_map.127 = (bf16[16,512]{1,0:T(8,128)(2,1)}, bf16[16,512]{1,0:T(8,128)(2,1)}, bf16[16,512]{1,0:T(8,128)(2,1)}, bf16[16,512]{1,0:T(8,128)(2,1)}, f32[1,16]{1,0:T(1,128)}) custom-call(f32[40,128]{1,0:T(8,128)S(1)} %get-tuple-element.25.rates_ref, f32[64,128]{1,0:T(8,128)S(1)} %get-tuple-element.26.starts_ref, f32[64,128]{1,0:T(8,128)S(1)} %get-tuple-element.27.ends_ref, ...), custom_call_target="tpu_custom_call" | custom-call | flops 20000000 | bytes 1000000 | tf_op jit(solution)/shard_map/pallas_call | solution.py:345
  15.0 0.0 collective-permute-done.other_ref
  15.0 0.5 %shard_map.129 = (f32[1,16]{1,0:T(1,128)}, f32[1,16]{1,0:T(1,128)}) custom-call(f32[1,16]{1,0:T(1,128)S(1)} %get-tuple-element.28.refs_0_.memory_ref, f32[1,16]{1,0:T(1,128)S(1)} %get-tuple-element.29.refs_1_.residue_ref, f32[8,128]{1,0:T(8,128)S(1)} %shard_map.128.mine_ref, f32[8,128]{1,0:T(8,128)S(1)} %collective-permute-done.other_ref), custom_call_target="tpu_custom_call" | custom-call | tf_op jit(solution)/shard_map/pallas_call | solution.py:354
Async XLA Ops:
  13.9 1.2 %collective-permute-start = (f32[8,128]{1,0:T(8,128)S(1)}, f32[8,128]{1,0:T(8,128)S(1)}, u32[]{:S(2)}, u32[]{:S(2)}) collective-permute-start(f32[8,128]{1,0:T(8,128)S(1)} %shard_map.128.mine_ref), channel_id=1, source_target_pairs={{0,1},{1,0},{2,3},{3,2},{4,5},{5,4},{6,7},{7,6},{8,9},{9,8},{10,11... | collective-permute-start | bytes 12296 | tf_op jit(solution)/shard_map/ppermute | solution.py:342

commit v9 on v8

--- a/solution.py
+++ b/solution.py
@@ -125,7 +125,7 @@
 def make_states(*refs):
     sources, (out_ref, rates_ref, starts_ref, ends_ref, *copies), arrived = refs[:7], refs[7:18], refs[18]
     moves = [pltpu.make_async_copy(*ends, arrived.at[i]) for i, ends in enumerate(zip(sources, copies))]
-    for i in (0, 3, 5, 6, 4, 1, 2):
+    for i in (0, 6, 4, 3, 5, 1, 2):
         moves[i].start()
     memory_ref, _, _, x_ref, q_ref, k_ref, d_ref = copies
     modes = memory_ref.shape[1]
@@ -144,14 +144,15 @@
     rates_ref[0:1] = leap
     rates_ref[1:2] = leap * (local_len * inv_row)
     rates_ref[2:3] = inv_row
+    rates_ref[3:4, :modes] = jnp.sqrt(2.0 / memory_ref[...])
     rates_ref[8 : 8 + modes] = decay_in
     rates_ref[8 + modes :] = decay_out
+    moves[6].wait()
+    moves[4].wait()
+    grads = by_chunk(d_ref) * by_chunk(q_ref)
     moves[3].wait()
     moves[5].wait()
     values = by_chunk(x_ref) * by_chunk(k_ref)
-    moves[6].wait()
-    moves[4].wait()
-    grads = by_chunk(d_ref) * by_chunk(q_ref)
     outer = contract(left_split(values, axis=0), right_split(grads, axis=0), 0, 0)
     outer = jnp.where(iota(outer.shape, 1) >= iota(outer.shape, 0), outer, 0.0)
     turn = (iota(outer.shape, 1) + iota(outer.shape, 0)) % LANES
@@ -245,10 +246,10 @@
     sums_ref[...] = sum([roll(sums, shift) for shift in range(modes, LANES, modes)], sums)
 
 
-def filter_grads(total, memory_ref, residue_ref, mine_ref, other_ref, *refs):
+def filter_grads(total, rates_ref, residue_ref, mine_ref, other_ref, *refs):
     results, scratch, sent = refs[:2], refs[2:4], refs[4]
-    modes = memory_ref.shape[1]
-    scale = jnp.sqrt(2.0 / memory_ref[...]) / math.sqrt(total)
+    modes = residue_ref.shape[1]
+    scale = rates_ref[3:4, :modes] * (1.0 / math.sqrt(total))
     sums = mine_ref[...] + other_ref[...]
     sum_zero, sum_one = sums[0:1, :modes], sums[1:2, :modes]
     scratch[0][...] = scale * sum_zero
@@ -357,7 +358,7 @@
         out_specs=[in_hbm] * 2,
         scratch_shapes=[*[pltpu.VMEM(*shape) for shape in small], pltpu.SemaphoreType.DMA((2,))],
         compiler_params=params,
-    )(copied[0], copied[1], sums, other)
+    )(rates, copied[1], sums, other)
     return (*results[:4], results[4][0], filters[0][0], filters[1][0])
 
 

time: 15.8 us -> 15.8 us (level)
  no operation moved by 1% of the time
where the time goes in v9:
time: 15.8 us; the launch traced here: 15.6 us
  blocking collectives  11.9 us (75%)
  Pallas kernels  3 us (19%)
  between operations  0.65 us (4%)
    all_to_all x1, blocking collectives, per_device(): lax.all_to_all(mine.reshape(peers, BLOCK, 1, LANES), AXES, 0, 0, axis_ind...  11.9 us
    pallas_call x1, Pallas kernels, per_device(): pl.pallas_call(make_states, in_specs=[in_hbm] * 7, out_shape=[jax.ShapeDt...  1.26 us
    pallas_call x1, Pallas kernels, per_device(): pl.pallas_call(functools.partial(finish, seq_size, ch_size), out_shape=[j...  1.1 us
    pallas_call x1, Pallas kernels, per_device(): pl.pallas_call(functools.partial(filter_grads, ch_size * channels * seq_s...  0.54 us
  transfers between devices with their start and end apart: 1, of which 0 were waited for; matrix products, arithmetic and copies ran while one was open for 0% of the time, Pallas kernels for 7%

profile of v9, /device:TPU:0, one launch (start us, length us, event | category | flops | bytes accessed | tf_op | source)
XLA Modules:
  0.0 15.6 jit_solution(12177520127773974005)
XLA Ops:
  0.6 1.3 %shard_map.126 = (f32[144,128]{1,0:T(8,128)S(1)}, f32[40,128]{1,0:T(8,128)S(1)}, f32[64,128]{1,0:T(8,128)S(1)}, f32[64,128]{1,0:T(8,128)S(1)}, f32[1,16]{1,0:T(1...) custom-call(f32[1,16]{1,0:T(1,128)} %bitcast.11, ...), custom_call_target="tpu_custom_call" | custom-call | tf_op jit(solution)/shard_map/pallas_call | solution.py:325
  1.9 11.9 %all_to_all.5 = f32[16,9,1,128]{3,2,1,0:T(1,128)S(1)} all-to-all(f32[16,9,1,128]{3,2,1,0:T(1,128)S(1)} %bitcast.10), channel_id=1, replica_groups={{23,3,19,27,7,31,11,15,20,0,16,24,4,28,8,12},{22,2,18,26,6,30,10,14,21,..., dimensions={0} | all-to-all | bytes 147456 | tf_op jit(solution)/shard_map/all_to_all | solution.py:336
  13.8 0.1 shard_map.128.mine_ref
  13.9 0.0 collective-permute-start
  13.9 1.1 %shard_map.127 = (bf16[16,512]{1,0:T(8,128)(2,1)}, bf16[16,512]{1,0:T(8,128)(2,1)}, bf16[16,512]{1,0:T(8,128)(2,1)}, bf16[16,512]{1,0:T(8,128)(2,1)}, f32[1,16]{1,0:T(1,128)}) custom-call(f32[40,128]{1,0:T(8,128)S(1)} %get-tuple-element.25.rates_ref, f32[64,128]{1,0:T(8,128)S(1)} %get-tuple-element.26.starts_ref, f32[64,128]{1,0:T(8,128)S(1)} %get-tuple-element.27.ends_ref, ...), custom_call_target="tpu_custom_call" | custom-call | flops 20000000 | bytes 1000000 | tf_op jit(solution)/shard_map/pallas_call | solution.py:346
  15.0 0.0 collective-permute-done.other_ref
  15.1 0.5 %shard_map.129 = (f32[1,16]{1,0:T(1,128)}, f32[1,16]{1,0:T(1,128)}) custom-call(f32[40,128]{1,0:T(8,128)S(1)} %get-tuple-element.25.rates_ref, f32[1,16]{1,0:T(1,128)S(1)} %get-tuple-element.29.refs_1_.residue_ref, f32[8,128]{1,0:T(8,128)S(1)} %shard_map.128.mine_ref, f32[8,128]{1,0:T(8,128)S(1)} %collective-permute-done.other_ref), custom_call_target="tpu_custom_call" | custom-call | tf_op jit(solution)/shard_map/pallas_call | solution.py:355
Async XLA Ops:
  13.9 1.2 %collective-permute-start = (f32[8,128]{1,0:T(8,128)S(1)}, f32[8,128]{1,0:T(8,128)S(1)}, u32[]{:S(2)}, u32[]{:S(2)}) collective-permute-start(f32[8,128]{1,0:T(8,128)S(1)} %shard_map.128.mine_ref), channel_id=1, source_target_pairs={{0,1},{1,0},{2,3},{3,2},{4,5},{5,4},{6,7},{7,6},{8,9},{9,8},{10,11... | collective-permute-start | bytes 12296 | tf_op jit(solution)/shard_map/ppermute | solution.py:343

commit v10 on v8

--- a/solution.py
+++ b/solution.py
@@ -240,8 +240,8 @@
         carry = lax.fori_loop(0, seq_size, pairs, carry)
     sums = [jnp.sum(carry[0][i] + carry[1][i], axis=0, keepdims=True) for i in (2, 3)]
     extras = jnp.sum(strided(all_ref, BLOCK - 1, chips * seq_size, BLOCK), axis=0, keepdims=True)
-    kind = iota((8, LANES), 0)
-    sums = jnp.where(kind == 0, sums[0], sums[1]) + jnp.where(iota((8, LANES), 1) // modes == kind, extras, 0.0)
+    kind = iota((2, LANES), 0)
+    sums = jnp.where(kind == 0, sums[0], sums[1]) + jnp.where(iota((2, LANES), 1) // modes == kind, extras, 0.0)
     sums_ref[...] = sum([roll(sums, shift) for shift in range(modes, LANES, modes)], sums)
 
 
@@ -336,7 +336,7 @@
     everyone = everyone.reshape(peers * BLOCK, LANES)
     sums = pl.pallas_call(
         functools.partial(pair_sums, seq_size, chips),
-        out_shape=jax.ShapeDtypeStruct((8, LANES), F32),
+        out_shape=jax.ShapeDtypeStruct((2, LANES), F32),
         compiler_params=params,
     )(rates, everyone)
     other = lax.ppermute(sums, "ch", [(i, i ^ 1) for i in range(ch_size)])

time: 15.8 us -> 15.8 us (level)
  no operation moved by 1% of the time
where the time goes in v10:
time: 15.8 us; the launch traced here: 15.6 us
  blocking collectives  11.9 us (75%)
  Pallas kernels  3.01 us (19%)
  between operations  0.65 us (4%)
    all_to_all x1, blocking collectives, per_device(): lax.all_to_all(mine.reshape(peers, BLOCK, 1, LANES), AXES, 0, 0, axis_ind...  11.9 us
    pallas_call x1, Pallas kernels, per_device(): pl.pallas_call(make_states, in_specs=[in_hbm] * 7, out_shape=[jax.ShapeDt...  1.26 us
    pallas_call x1, Pallas kernels, per_device(): pl.pallas_call(functools.partial(finish, seq_size, ch_size), out_shape=[j...  1.09 us
    pallas_call x1, Pallas kernels, per_device(): pl.pallas_call(functools.partial(filter_grads, ch_size * channels * seq_s...  0.55 us
  transfers between devices with their start and end apart: 1, of which 0 were waited for; matrix products, arithmetic and copies ran while one was open for 0% of the time, Pallas kernels for 7%

profile of v10, /device:TPU:0, one launch (start us, length us, event | category | flops | bytes accessed | tf_op | source)
XLA Modules:
  0.0 15.6 jit_solution(693826340686905463)
XLA Ops:
  0.6 1.3 %shard_map.126 = (f32[144,128]{1,0:T(8,128)S(1)}, f32[40,128]{1,0:T(8,128)S(1)}, f32[64,128]{1,0:T(8,128)S(1)}, f32[64,128]{1,0:T(8,128)S(1)}, f32[1,16]{1,0:T(1...) custom-call(f32[1,16]{1,0:T(1,128)} %bitcast.11, ...), custom_call_target="tpu_custom_call" | custom-call | tf_op jit(solution)/shard_map/pallas_call | solution.py:324
  1.9 11.9 %all_to_all.5 = f32[16,9,1,128]{3,2,1,0:T(1,128)S(1)} all-to-all(f32[16,9,1,128]{3,2,1,0:T(1,128)S(1)} %bitcast.10), channel_id=1, replica_groups={{23,3,19,27,7,31,11,15,20,0,16,24,4,28,8,12},{22,2,18,26,6,30,10,14,21,..., dimensions={0} | all-to-all | bytes 147456 | tf_op jit(solution)/shard_map/all_to_all | solution.py:335
  13.8 0.1 shard_map.128.mine_ref
  13.9 0.0 collective-permute-start
  13.9 1.1 %shard_map.127 = (bf16[16,512]{1,0:T(8,128)(2,1)}, bf16[16,512]{1,0:T(8,128)(2,1)}, bf16[16,512]{1,0:T(8,128)(2,1)}, bf16[16,512]{1,0:T(8,128)(2,1)}, f32[1,16]{1,0:T(1,128)}) custom-call(f32[40,128]{1,0:T(8,128)S(1)} %get-tuple-element.25.rates_ref, f32[64,128]{1,0:T(8,128)S(1)} %get-tuple-element.26.starts_ref, f32[64,128]{1,0:T(8,128)S(1)} %get-tuple-element.27.ends_ref, ...), custom_call_target="tpu_custom_call" | custom-call | flops 20000000 | bytes 1000000 | tf_op jit(solution)/shard_map/pallas_call | solution.py:345
  15.0 0.0 collective-permute-done.other_ref
  15.0 0.5 %shard_map.129 = (f32[1,16]{1,0:T(1,128)}, f32[1,16]{1,0:T(1,128)}) custom-call(f32[1,16]{1,0:T(1,128)S(1)} %get-tuple-element.28.refs_0_.memory_ref, f32[1,16]{1,0:T(1,128)S(1)} %get-tuple-element.29.refs_1_.residue_ref, f32[2,128]{1,0:T(2,128)S(1)} %shard_map.128.mine_ref, f32[2,128]{1,0:T(2,128)S(1)} %collective-permute-done.other_ref), custom_call_target="tpu_custom_call" | custom-call | tf_op jit(solution)/shard_map/pallas_call | solution.py:354
Async XLA Ops:
  13.9 1.1 %collective-permute-start = (f32[2,128]{1,0:T(2,128)S(1)}, f32[2,128]{1,0:T(2,128)S(1)}, u32[]{:S(2)}, u32[]{:S(2)}) collective-permute-start(f32[2,128]{1,0:T(2,128)S(1)} %shard_map.128.mine_ref), channel_id=1, source_target_pairs={{0,1},{1,0},{2,3},{3,2},{4,5},{5,4},{6,7},{7,6},{8,9},{9,8},{10,11... | collective-permute-start | bytes 3080 | tf_op jit(solution)/shard_map/ppermute | solution.py:342

commit v11 on v8

--- a/solution.py
+++ b/solution.py
@@ -330,7 +330,7 @@
     )(*arguments)
     groups = [
         [s * ch_size + chip * CORES + (core + chip) % CORES for chip in chip_ranks(chips) for s in seq_ranks(seq_size)]
-        for core in range(CORES)
+        for core in reversed(range(CORES))
     ]
     everyone = lax.all_to_all(mine.reshape(peers, BLOCK, 1, LANES), AXES, 0, 0, axis_index_groups=groups)
     everyone = everyone.reshape(peers * BLOCK, LANES)

time: 15.8 us -> 15.8 us (level)
  no operation moved by 1% of the time
where the time goes in v11:
time: 15.8 us; the launch traced here: 15.6 us
  blocking collectives  11.9 us (75%)
  Pallas kernels  3.01 us (19%)
  between operations  0.65 us (4%)
    all_to_all x1, blocking collectives, per_device(): lax.all_to_all(mine.reshape(peers, BLOCK, 1, LANES), AXES, 0, 0, axis_ind...  11.9 us
    pallas_call x1, Pallas kernels, per_device(): pl.pallas_call(make_states, in_specs=[in_hbm] * 7, out_shape=[jax.ShapeDt...  1.26 us
    pallas_call x1, Pallas kernels, per_device(): pl.pallas_call(functools.partial(finish, seq_size, ch_size), out_shape=[j...  1.09 us
    pallas_call x1, Pallas kernels, per_device(): pl.pallas_call(functools.partial(filter_grads, ch_size * channels * seq_s...  0.55 us
  transfers between devices with their start and end apart: 1, of which 0 were waited for; matrix products, arithmetic and copies ran while one was open for 0% of the time, Pallas kernels for 7%

profile of v11, /device:TPU:0, one launch (start us, length us, event | category | flops | bytes accessed | tf_op | source)
XLA Modules:
  0.0 15.6 jit_solution(4019318217567077642)
XLA Ops:
  0.6 1.3 %shard_map.126 = (f32[144,128]{1,0:T(8,128)S(1)}, f32[40,128]{1,0:T(8,128)S(1)}, f32[64,128]{1,0:T(8,128)S(1)}, f32[64,128]{1,0:T(8,128)S(1)}, f32[1,16]{1,0:T(1...) custom-call(f32[1,16]{1,0:T(1,128)} %bitcast.11, ...), custom_call_target="tpu_custom_call" | custom-call | tf_op jit(solution)/shard_map/pallas_call | solution.py:324
  1.9 11.9 %all_to_all.5 = f32[16,9,1,128]{3,2,1,0:T(1,128)S(1)} all-to-all(f32[16,9,1,128]{3,2,1,0:T(1,128)S(1)} %bitcast.10), channel_id=1, replica_groups={{22,2,18,26,6,30,10,14,21,1,17,25,5,29,9,13},{23,3,19,27,7,31,11,15,20,..., dimensions={0} | all-to-all | bytes 147456 | tf_op jit(solution)/shard_map/all_to_all | solution.py:335
  13.8 0.1 shard_map.128.mine_ref
  13.9 0.0 collective-permute-start
  13.9 1.1 %shard_map.127 = (bf16[16,512]{1,0:T(8,128)(2,1)}, bf16[16,512]{1,0:T(8,128)(2,1)}, bf16[16,512]{1,0:T(8,128)(2,1)}, bf16[16,512]{1,0:T(8,128)(2,1)}, f32[1,16]{1,0:T(1,128)}) custom-call(f32[40,128]{1,0:T(8,128)S(1)} %get-tuple-element.25.rates_ref, f32[64,128]{1,0:T(8,128)S(1)} %get-tuple-element.26.starts_ref, f32[64,128]{1,0:T(8,128)S(1)} %get-tuple-element.27.ends_ref, ...), custom_call_target="tpu_custom_call" | custom-call | flops 20000000 | bytes 1000000 | tf_op jit(solution)/shard_map/pallas_call | solution.py:345
  15.0 0.0 collective-permute-done.other_ref
  15.0 0.5 %shard_map.129 = (f32[1,16]{1,0:T(1,128)}, f32[1,16]{1,0:T(1,128)}) custom-call(f32[1,16]{1,0:T(1,128)S(1)} %get-tuple-element.28.refs_0_.memory_ref, f32[1,16]{1,0:T(1,128)S(1)} %get-tuple-element.29.refs_1_.residue_ref, f32[8,128]{1,0:T(8,128)S(1)} %shard_map.128.mine_ref, f32[8,128]{1,0:T(8,128)S(1)} %collective-permute-done.other_ref), custom_call_target="tpu_custom_call" | custom-call | tf_op jit(solution)/shard_map/pallas_call | solution.py:354
Async XLA Ops:
  13.9 1.2 %collective-permute-start = (f32[8,128]{1,0:T(8,128)S(1)}, f32[8,128]{1,0:T(8,128)S(1)}, u32[]{:S(2)}, u32[]{:S(2)}) collective-permute-start(f32[8,128]{1,0:T(8,128)S(1)} %shard_map.128.mine_ref), channel_id=1, source_target_pairs={{0,1},{1,0},{2,3},{3,2},{4,5},{5,4},{6,7},{7,6},{8,9},{9,8},{10,11... | collective-permute-start | bytes 12296 | tf_op jit(solution)/shard_map/ppermute | solution.py:342
